TPU v7x, 128 devices: a whole 4x4x4 slice. The times are simulated.
128 devices in a mesh: pipe: 4 (over y_hi, core), fsdp: 32 (over x, z, y_lo).
Axes of the slice: x: 4, y: 4 (y_hi: 2, y_lo: 2; y = y_hi * 2 + y_lo), z: 4, core: 2. Of those that a mesh axis runs over, the one named last changes fastest.
Arguments:
- inputs: bfloat16 [4, 2048, 8192], P(None, 'fsdp'), may hold values from -60 to 60
- cotangent: bfloat16 [4, 2048, 8192], P(None, 'fsdp'), may hold values from -0.25 to 0.25
- right_factor: bfloat16 [4, 64, 128, 128], P('pipe', 'fsdp'), may hold values from -0.5 to 0.5
- left_factor: bfloat16 [4, 64, 128, 128], P('pipe', 'fsdp'), may hold values from -0.5 to 0.5
- norm_gain: bfloat16 [4, 8192], P('pipe', 'fsdp'), may hold values from 0.25 to 1.75
Outputs:
- grad_right: float32 [4, 64, 128, 128], P('pipe', 'fsdp')
- grad_left: float32 [4, 64, 128, 128], P('pipe', 'fsdp')
- grad_gain: float32 [4, 8192], P('pipe', 'fsdp')
All inputs are finite; a program needn't handle non-finite values.
Results may differ from a plain program's by a relative error of at most 0.034.
Values may be sent and summed in bfloat16 or wider, within the bound.
No kernel may reach another device: no remote copies, remote signals or barrier semaphores. Data moves between devices by JAX's collectives and lax.ppermute only.
A program may use at most 192 MiB of HBM per device.

v0:
```python
import functools

import jax
import jax.numpy as jnp
from jax import lax
from jax.experimental import pallas as pl
from jax.experimental.pallas import tpu as pltpu
from jax.sharding import Mesh, PartitionSpec as P

EPSILON = 1e-05
TANH_SLOPE = 0.7978845608028654
CUBIC_TERM = 0.044715

BF = jnp.bfloat16
F32 = jnp.float32
HI = lax.Precision.HIGHEST
SWAP = ((0, 1), (1, 0))
YS = ("yh", "yl")
VMEM_LIMIT = 24 * 1024 * 1024

NB = 64
BS = 128
D = NB * BS
HB = NB // 2
ROWS = HB * BS
HALF = ROWS // 2
TOK = 128
STAT = 16
FORWARD = (65, 64)
BACKWARD = (33, 32)
GRID = 4
BPC = HB // GRID


def mm(a, b):
    return lax.dot_general(a, b, (((1,), (0,)), ((), ())), preferred_element_type=F32)


def mm_ta(a, b):
    return mm(a.T, b)


def mm_tb(a, b):
    return mm(a, b.T)


def mm_exact(a, b, dims=((1,), (0,))):
    return lax.dot_general(a, b, (dims, ((), ())), precision=HI, preferred_element_type=F32)


def iota2(dim):
    return lax.broadcasted_iota(jnp.int32, (BS, BS), dim)


def column_source(dp, q):
    rel = dp // 64
    return ((dp // 32) % 2) * 64 + 2 * (dp % 32) + (rel + q - 2 * rel * q)


def row_source(cp, q):
    rel = cp // 64
    return 4 * ((cp % 64) // 2) + 2 * (rel + q - 2 * rel * q) + cp % 2


def stat_rows(value):
    hi = value.astype(BF)
    rest = value - hi.astype(F32)
    mid = rest.astype(BF)
    lo = (rest - mid.astype(F32)).astype(BF)
    row = lax.broadcasted_iota(jnp.int32, (STAT, TOK), 0)
    out = jnp.where(row == 0, hi.astype(F32), jnp.where(row == 1, mid.astype(F32), lo.astype(F32)))
    return jnp.where(row < 3, out, 0.0).astype(BF)


def stat_total(own_ref, recv_ref):
    rows = recv_ref[pl.ds(HALF, STAT), :].astype(F32)
    return own_ref[0:1, :] + jnp.sum(rows, axis=0, keepdims=True)


def folded(value):
    return jnp.sum(value.reshape(BS // 8, 8, TOK), axis=0)


def back(index, steps):
    return (index + (4 - steps)) % 4


def blocks(place_ref):
    for sx in range(4):
        xm = back(place_ref[2], sx)
        for sz in range(4):
            zm = back(place_ref[3], sz)
            for ym in range(2):
                yield sx, sz, xm, zm, ym, xm * 8 + zm * 2 + ym


def slot(layer, at, yl):
    return layer * 8 + at * 2 + yl


def rows_of(m):
    return pl.ds(pl.multiple_of(m * BS, BS), BS)


def prep_kernel(place_ref, right_ref, left_ref, gain_ref, keep_ref, send_ref):
    core = place_ref[0]
    for dst, q in ((keep_ref, core), (send_ref, 1 - core)):
        gain_row = gain_ref[q].astype(F32)
        diag = jnp.where(iota2(0) == iota2(1), gain_row, 0.0).astype(BF)
        scaled = mm(diag, right_ref[q]).astype(BF)
        pick = (iota2(0) == column_source(iota2(1), q)).astype(F32).astype(BF)
        dst[0] = mm(scaled, pick).astype(BF)
        pick = (iota2(1) == row_source(iota2(0), q)).astype(F32).astype(BF)
        dst[1] = mm(pick, left_ref[q]).astype(BF)


def taken(pieces, s, k, size, at):
    if s == 2:
        return pieces[2 + k // 2][(k // 2) * (size // 8) + (k % 2) * size + at]
    return pieces[s + s // 3][k * size + at]


def gather_y_kernel(place_ref, p0, p1, p2, p3, right_ref, left_ref):
    core = place_ref[0]
    for s, piece in enumerate((p0, p1, p2, p3)):
        y = back(place_ref[4], s)
        for k in range(2):
            layer = (y // 2) * 2 + (core + k) % 2
            right_ref[layer * 2 + y % 2] = piece[k, 0]
            left_ref[layer * 2 + y % 2] = piece[k, 1]


def gather_pair_kernel(place_ref, *refs):
    for pieces, index, out in ((refs[:5], 3, refs[10]), (refs[5:10], 2, refs[11])):
        for s in range(4):
            at = back(place_ref[index], s)
            for k in range(4):
                for yl in range(2):
                    out[k * 8 + at * 2 + yl] = taken(pieces, s, k, 2, yl)


def tokens_kernel(place_ref, in_ref, cot_ref, x_ref, grad_ref, stat_ref):
    core = place_ref[0]
    base = pl.program_id(0) * BPC
    total = jnp.zeros((8, TOK), F32)
    for i in range(BPC):
        lanes = pl.ds(pl.multiple_of((2 * i + core) * BS, BS), BS)
        x = in_ref[:, :, lanes].reshape(TOK, BS).astype(F32).T
        x_ref[rows_of(base + i), :] = x.astype(BF)
        total = total + folded(x * x)
        grad_ref[rows_of(base + i), :] = cot_ref[:, :, lanes].reshape(TOK, BS).astype(F32).T.astype(BF)
    total = jnp.broadcast_to(jnp.sum(total, axis=0, keepdims=True), (8, TOK))

    @pl.when(pl.program_id(0) == 0)
    def _():
        stat_ref[...] = jnp.zeros_like(stat_ref)

    stat_ref[...] += total


def put_forward(scr, m, product):
    for part in range(2):
        for h in range(2):
            scr[part, pl.ds(m * 2 + h, 32, stride=FORWARD[0]), :] = product[part * 64 + h * 32 :][:32]


def put_backward(scr, m, product):
    for part in range(2):
        scr[part, pl.ds(m, 64, stride=BACKWARD[0]), :] = product[part * 64 :][:64]


def flush(runs, scr, total, own_ref, send_ref, stat_ref):
    pitch, used = runs
    for i in range(HALF // used):
        own_ref[pl.ds(i * used, used), :] = scr[0, pl.ds(i * pitch, used), :].astype(BF)
        send_ref[pl.ds(i * used, used), :] = scr[1, pl.ds(i * pitch, used), :].astype(BF)
    send_ref[pl.ds(HALF, STAT), :] = stat_rows(total)
    stat_ref[...] = jnp.broadcast_to(total, stat_ref.shape)


def gelu_parts(v):
    sq = v * v
    t = jnp.tanh(v * (TANH_SLOPE + (TANH_SLOPE * CUBIC_TERM) * sq))
    half = 0.5 * t + 0.5
    slope = half + (v * (1.0 - t * t)) * (0.5 * TANH_SLOPE + (1.5 * TANH_SLOPE * CUBIC_TERM) * sq)
    return v * half, slope


def rms_of(own_stat, recv_ref):
    return lax.rsqrt(stat_total(own_stat, recv_ref) * (1.0 / D) + EPSILON)


def permuted_block(own_ref, recv_ref, m, rms):
    rows = pl.ds(pl.multiple_of(m * 64, 64), 64)
    both = jnp.concatenate([own_ref[rows, :], recv_ref[rows, :]], axis=0)
    if rms is None:
        return both
    return (both.astype(F32) * rms).astype(BF)


def start_kernel(place_ref, x_ref, st_ref, w0, w1, w2, w3, w4, own_ref, send_ref, stat_ref, scr):
    rights = (w0, w1, w2, w3, w4)
    for sx, sz, xm, zm, ym, m in blocks(place_ref):
        put_forward(scr, m, mm_ta(taken(rights, sx, 0, 8, zm * 2 + ym), x_ref[rows_of(m), :]))
    flush(FORWARD, scr, st_ref[0:1, :], own_ref, send_ref, stat_ref)


def forward_kernel(
    layer, place_ref, uo_ref, ur_ref, us_ref, x_ref, l0, l1, l2, l3, l4, w0, w1, w2, w3, w4,
    xn_ref, slope_ref, perm_ref, rms_ref, own_ref, send_ref, stat_ref, scr,
):
    lefts, rights = (l0, l1, l2, l3, l4), (w0, w1, w2, w3, w4)
    rms = rms_of(us_ref, ur_ref)
    rms_ref[...] = jnp.broadcast_to(rms, rms_ref.shape)
    total = jnp.zeros((8, TOK), F32)
    for sx, sz, xm, zm, ym, m in blocks(place_ref):
        rows = rows_of(m)
        perm = permuted_block(uo_ref, ur_ref, m, rms)
        perm_ref[rows, :] = perm
        value, slope = gelu_parts(mm_ta(taken(lefts, sz, layer, 8, xm * 2 + ym), perm))
        slope_ref[rows, :] = slope.astype(BF)
        xb = (x_ref[rows, :].astype(F32) + value).astype(BF)
        xn_ref[rows, :] = xb
        x = xb.astype(F32)
        total = total + folded(x * x)
        put_forward(scr, m, mm_ta(taken(rights, sx, layer + 1, 8, zm * 2 + ym), xb))
    flush(FORWARD, scr, jnp.sum(total, axis=0, keepdims=True), own_ref, send_ref, stat_ref)


def left_chain(grad, slope, perm, left, rms, m, scr):
    grad_pre = (grad.astype(F32) * slope).astype(BF)
    grad_perm = mm(left, grad_pre)
    put_backward(scr, m, grad_perm * rms)
    return grad_pre, folded(grad_perm * perm.astype(F32))


def turn_kernel(
    layer, place_ref, uo_ref, ur_ref, us_ref, grad_ref, l0, l1, l2, l3, l4,
    rms_ref, perm_ref, pre_ref, own_ref, send_ref, stat_ref, scr,
):
    lefts = (l0, l1, l2, l3, l4)
    rms = rms_of(us_ref, ur_ref)
    rms_ref[...] = jnp.broadcast_to(rms, rms_ref.shape)
    total = jnp.zeros((8, TOK), F32)
    for sx, sz, xm, zm, ym, m in blocks(place_ref):
        rows = rows_of(m)
        perm = permuted_block(uo_ref, ur_ref, m, rms)
        perm_ref[rows, :] = perm
        left = taken(lefts, sz, layer, 8, xm * 2 + ym)
        slope = gelu_parts(mm_ta(left, perm))[1]
        pre_ref[rows, :], add = left_chain(grad_ref[rows, :], slope, perm, left, rms, m, scr)
        total = total + add
    flush(BACKWARD, scr, jnp.sum(total, axis=0, keepdims=True), own_ref, send_ref, stat_ref)


def backward_kernel(layer, *refs):
    place_ref, go_ref, gr_ref, gs_ref, rms_ref, rms_below_ref, x_ref, grad_ref, slope_ref, perm_ref = refs[:10]
    rights, lefts, refs = refs[10:15], refs[15:20], refs[20:]
    pre_ref, own_ref, send_ref, stat_ref = refs[:4]
    new_ref, scr = refs[4] if layer > 1 else None, refs[-1]
    below = layer - 1
    rms = rms_ref[0:1, :]
    rms_below = rms_below_ref[0:1, :]
    coef = stat_total(gs_ref, gr_ref) * (rms * rms * (1.0 / D))
    total = jnp.zeros((8, TOK), F32)
    for sx, sz, xm, zm, ym, m in blocks(place_ref):
        rows = rows_of(m)
        gf = permuted_block(go_ref, gr_ref, m, None)
        grad = grad_ref[rows, :].astype(F32) + mm(taken(rights, sx, layer, 8, zm * 2 + ym), gf)
        grad = (grad - x_ref[rows, :].astype(F32) * coef).astype(BF)
        if new_ref is not None:
            new_ref[rows, :] = grad
        left = taken(lefts, sz, below, 8, xm * 2 + ym)
        pre_ref[rows, :], add = left_chain(
            grad, slope_ref[rows, :].astype(F32), perm_ref[rows, :], left, rms_below, m, scr
        )
        total = total + add
    flush(BACKWARD, scr, jnp.sum(total, axis=0, keepdims=True), own_ref, send_ref, stat_ref)


def factor_kernel(right_layer, left_layer, n_old, *refs):
    refs = refs[n_old:]
    place_ref, refs = refs[0], refs[1:]
    if right_layer is not None:
        (go_ref, gr_ref, x_ref), refs = refs[:3], refs[3:]
    if left_layer is not None:
        (perm_ref, pre_ref), refs = refs[:2], refs[2:]
    for sx, sz, xm, zm, ym, m in blocks(place_ref):
        rows = rows_of(m)
        if right_layer is not None:
            gf = permuted_block(go_ref, gr_ref, m, None)
            refs[sx][slot(right_layer, zm, ym)] = mm_tb(x_ref[rows, :], gf).astype(BF)
        if left_layer is not None:
            refs[sz - 4][slot(left_layer, xm, ym)] = mm_tb(perm_ref[rows, :], pre_ref[rows, :]).astype(BF)


def added(parts):
    parts = [p.astype(F32) for p in parts]
    total = parts[0] + parts[1]
    return total + parts[2] if len(parts) == 3 else total + (parts[2] + parts[3]) if len(parts) == 4 else total


def pass_kernel(place_ref, down_ref, up_ref, lo_ref, hi_ref, down_out, up_out):
    del place_ref
    for i in range(16):
        down_out[i] = added((down_ref[i], lo_ref[i])).astype(BF)
        down_out[16 + i] = down_ref[16 + i]
        up_out[i] = up_ref[i]
        up_out[16 + i] = added((up_ref[16 + i], hi_ref[i])).astype(BF)


def sum_pair_kernel(place_ref, *refs):
    sources, outs = refs[:6], refs[6:]
    for side, index in ((0, 3), (1, 2)):
        slabs = sources[side * 3 :][:3]
        for s in range(4):
            at = back(place_ref[index], s)
            for yl in range(2):
                for layer in range(4):
                    outs[side * 4 + s][yl, layer] = added([t[slot(layer, at, yl)] for t in slabs]).astype(BF)


def sum_ring_kernel(place_ref, *refs):
    sources, outs = refs[:8], refs[8:]
    for side in range(2):
        slabs = sources[side * 4 :][:4]
        for s in range(4):
            y = back(place_ref[4], s)
            for k in range(2):
                outs[s][k, side] = added([t[y % 2, (y // 2) * 2 + k] for t in slabs]).astype(BF)


def sum_y_kernel(place_ref, p0, p1, p2, p3, keep_ref, send_ref):
    core = place_ref[0]
    for dst, k in ((keep_ref, core), (send_ref, 1 - core)):
        for side in range(2):
            dst[side] = added([t[k, side] for t in (p0, p1, p2, p3)])


def finish_kernel(place_ref, keep_ref, recv_ref, right_ref, gain_ref, gr_ref, gl_ref, gg_ref):
    core = place_ref[0]
    for src, q in ((keep_ref, core), (recv_ref, 1 - core)):
        pick = (iota2(1) == column_source(iota2(0), q)).astype(F32)
        raw = mm_exact(src[0], pick)
        diag = jnp.where(iota2(0) == iota2(1), gain_ref[q].astype(F32), 0.0)
        gr_ref[q] = mm_exact(diag, raw)
        gg_ref[q] = mm_exact(jnp.ones((8, BS), F32), raw * right_ref[q].astype(F32), ((1,), (1,)))[0:1]
        pick = (iota2(0) == row_source(iota2(1), q)).astype(F32)
        gl_ref[q] = mm_exact(pick, src[1])


WHOLE = pl.BlockSpec(memory_space=pltpu.VMEM)
SCALARS = pl.BlockSpec(memory_space=pltpu.SMEM)
ANY = pl.BlockSpec(memory_space=pl.ANY)
TOKENS_SPEC = pl.BlockSpec((2, 64, D // GRID), lambda g, place: (place[1], 0, g))


def kept(*shape, dtype=BF):
    return pltpu.VMEM(shape, dtype)


U_OUT = (kept(HALF, TOK), kept(HALF + STAT, TOK), kept(8, TOK, dtype=F32))
ACT = kept(ROWS, TOK)
STATS = kept(8, TOK, dtype=F32)
SLAB = kept(32, BS, BS)
SCRATCH = (pltpu.VMEM((2, HALF + 64, TOK), F32),)


def call(kernel, place, ins, outs, scratch=(), old=()):
    vmem = [pltpu.with_memory_space_constraint(a, pltpu.VMEM) for a in (*old, *ins)]
    ins = (*vmem[: len(old)], place, *vmem[len(old) :])
    return pl.pallas_call(
        kernel,
        out_shape=outs,
        in_specs=[WHOLE] * len(old) + [SCALARS] + [WHOLE] * (len(ins) - len(old) - 1),
        out_specs=(WHOLE,) * len(outs),
        scratch_shapes=scratch,
        compiler_params=pltpu.CompilerParams(vmem_limit_bytes=VMEM_LIMIT),
    )(*ins)


def swapped(value):
    return lax.ppermute(value, "c", SWAP)


def ring(value, axes, steps):
    return lax.ppermute(value, axes, [(i, (i + steps) % 4) for i in range(4)])


def gathered(value, axes):
    return [value] + [ring(value, axes, s) for s in (1, 2, 3)]


def ring_gathered(value, axes):
    half = value.shape[0] // 2
    up, down = ring(value, axes, 1), ring(value, axes, -1)
    spare = half // 16
    return [value, up, ring(up[: half + spare], axes, 1), ring(down[half - spare :], axes, -1), down]


def scattered(slabs, axes):
    return [slabs[0]] + [ring(slabs[s], axes, -s) for s in (1, 2, 3)]


def ring_reduced(right_slabs, left_slabs, place):
    sides = ((right_slabs, "x"), (left_slabs, "z"))
    far = [(ring(slabs[2][:16], axes, -1), ring(slabs[2][16:], axes, 1)) for slabs, axes in sides]
    parts = []
    for (slabs, axes), got in zip(sides, far):
        down, up = call(pass_kernel, place, (slabs[1], slabs[3], *got), (SLAB, SLAB))
        parts += [slabs[0], ring(down, axes, -1), ring(up, axes, 1)]
    return parts


def per_device(inputs, cotangent, right_factor, left_factor, norm_gain):
    core, yh, yl = lax.axis_index("c"), lax.axis_index("yh"), lax.axis_index("yl")
    place = jnp.stack([core, yh, lax.axis_index("x"), lax.axis_index("z"), 2 * yh + yl]).astype(jnp.int32)
    right = right_factor[0]
    left = left_factor[0]
    gain = norm_gain.reshape(2, 1, BS)

    keep, send = call(prep_kernel, place, (right, left, gain), (kept(2, BS, BS),) * 2)
    mine = jnp.stack([keep, swapped(send)])
    stage = kept(2, 4, BS, BS)
    part = kept(8, BS, BS)
    all_right, all_left = call(gather_y_kernel, place, gathered(mine, YS), (part, part))
    firsts = call(
        gather_pair_kernel, place, ring_gathered(all_right, "z") + ring_gathered(all_left, "x"), (kept(32, BS, BS),) * 2
    )
    rights, lefts = ring_gathered(firsts[0], "x"), ring_gathered(firsts[1], "z")

    x, grad, st = pl.pallas_call(
        tokens_kernel,
        out_shape=(ACT, ACT, STATS),
        grid_spec=pltpu.PrefetchScalarGridSpec(
            num_scalar_prefetch=1, grid=(GRID,), in_specs=[TOKENS_SPEC] * 2, out_specs=(WHOLE,) * 3
        ),
        compiler_params=pltpu.CompilerParams(vmem_limit_bytes=VMEM_LIMIT),
    )(place, inputs, cotangent)

    uo, us, st = call(start_kernel, place, (x, st, *rights), U_OUT, SCRATCH)
    xs, slopes, perms, rmss = [x], [], [], []
    for layer in range(3):
        xn, slope, perm, rms, uo, us, st = call(
            functools.partial(forward_kernel, layer), place,
            (uo, swapped(us), st, xs[-1], *lefts, *rights),
            (ACT, ACT, ACT, STATS) + U_OUT, SCRATCH,
        )
        xs.append(xn)
        slopes.append(slope)
        perms.append(perm)
        rmss.append(rms)
    rms, perm, pre, uo, us, st = call(
        functools.partial(turn_kernel, 3), place, (uo, swapped(us), st, grad, *lefts), (STATS, ACT, ACT) + U_OUT, SCRATCH
    )
    perms.append(perm)
    rmss.append(rms)
    slabs = {"right": (), "left": ()}

    def factors(right_layer, left_layer, ins):
        sides = [side for side, layer in (("right", right_layer), ("left", left_layer)) if layer is not None]
        old, aliases = [], {}
        for n, side in enumerate(sides):
            for k, slab in enumerate(slabs[side]):
                aliases[len(old)] = 4 * n + k
                old.append(slab)
        outs = call_into(
            functools.partial(factor_kernel, right_layer, left_layer, len(old)), place, ins, (SLAB,) * (4 * len(sides)), (), old,
            aliases,
        )
        for n, side in enumerate(sides):
            slabs[side] = outs[4 * n : 4 * n + 4]

    factors(None, 3, (perm, pre))
    for layer in (3, 2, 1):
        below = layer - 1
        go, gr = uo, swapped(us)
        pre, uo, us, st, *grad = call(
            functools.partial(backward_kernel, layer), place,
            (go, gr, st, rmss[layer], rmss[below], xs[layer], *([grad] if layer == 3 else grad), slopes[below], perms[below],
             *rights, *lefts),
            (ACT,) + U_OUT + (ACT,) * (layer > 1), SCRATCH,
        )
        factors(layer, below, (go, gr, xs[layer], perms[below], pre))
    factors(0, None, (uo, swapped(us), xs[0]))
    outs = call(sum_pair_kernel, place, ring_reduced(slabs["right"], slabs["left"], place), (stage,) * 8)
    parts = scattered(outs[:4], "z") + scattered(outs[4:], "x")
    outs = call(sum_ring_kernel, place, parts, (kept(2, 2, BS, BS),) * 4)
    sums = kept(2, BS, BS, dtype=F32)
    keep, send = call(sum_y_kernel, place, scattered(outs, YS), (sums, sums))
    whole = jax.ShapeDtypeStruct((2, BS, BS), F32)
    grad_right, grad_left, grad_gain = call(
        finish_kernel, place, (keep, swapped(send), right, gain), (whole, whole, jax.ShapeDtypeStruct((2, 1, BS), F32))
    )
    return grad_right[None], grad_left[None], grad_gain.reshape(1, 2 * BS)


def call_into(kernel, place, ins, outs, scratch, old, aliases):
    vmem = [pltpu.with_memory_space_constraint(a, pltpu.VMEM) for a in (*old, *ins)]
    operands = (*vmem[: len(old)], place, *vmem[len(old) :])
    return pl.pallas_call(
        kernel,
        out_shape=outs,
        in_specs=[WHOLE] * len(old) + [SCALARS] + [WHOLE] * len(ins),
        out_specs=(WHOLE,) * len(outs),
        scratch_shapes=scratch,
        input_output_aliases=aliases,
        compiler_params=pltpu.CompilerParams(vmem_limit_bytes=VMEM_LIMIT),
    )(*operands)


def solution(mesh):
    parts = Mesh(mesh.devices.reshape(2, 2, 4, 4, 2), ("yh", "c", "x", "z", "yl"))
    pipe, fsdp = ("yh", "c"), ("x", "z", "yl")
    return jax.shard_map(
        per_device,
        mesh=parts,
        in_specs=(P(None, fsdp, None), P(None, fsdp, None), P(pipe, fsdp, None, None), P(pipe, fsdp, None, None), P(pipe, fsdp)),
        out_specs=(P(pipe, fsdp, None, None), P(pipe, fsdp, None, None), P(pipe, fsdp)),
        check_vma=False,
    )
```

profile of v0, /device:TPU:1, one launch (start us, length us, event | category | flops | bytes accessed | tf_op | source)
XLA Modules:
  0.0 211.1 jit_solution(11415177060404762928)
XLA Ops:
  6.5 2.9 %collective-permute-start.3 = (bf16[2,2,128,128]{3,2,1,0:T(8,128)(2,1)S(1)}, bf16[2,2,128,128]{3,2,1,0:T(8,128)(2,1)S(1)}, u32[]{:S(2)}, u32[]{:S(2)}) collective-permute-start(bf16[2,2,128,128]{3,2,1,0:T(8,128)(2,1)S(1)} %pad_maximum_fusion.p0), channel_id=1, source_target_pairs={{0,65},{1,0},{64,1},{65,64},{2,67},{3,2},{66,3},{67,66},{4,69},{5,... | collective-permute-start | bytes 393224 | tf_op jit(solution)/shard_map/ppermute | solution.py:387
  10.4 4.2 %collective-permute-done.3.p3 = bf16[2,2,128,128]{3,2,1,0:T(8,128)(2,1)S(1)} collective-permute-done((bf16[2,2,128,128]{3,2,1,0:T(8,128)(2,1)S(1)}, bf16[2,2,128,128]{3,2,1,0:T(8,128)(2,1)S(1)}, u32[]{:S(2)}, u32[]{:S(2)}) %collective-permute-start.3) | collective-permute-done | bytes 131104 | tf_op jit(solution)/shard_map/ppermute | solution.py:387
  15.3 3.8 %collective-permute-done.1.p1 = bf16[2,2,128,128]{3,2,1,0:T(8,128)(2,1)S(1)} collective-permute-done((bf16[2,2,128,128]{3,2,1,0:T(8,128)(2,1)S(1)}, bf16[2,2,128,128]{3,2,1,0:T(8,128)(2,1)S(1)}, u32[]{:S(2)}, u32[]{:S(2)}) %collective-permute-start.1) | collective-permute-done | bytes 131104 | tf_op jit(solution)/shard_map/ppermute | solution.py:387
  19.7 3.8 %collective-permute-start.6 = (bf16[8,128,128]{2,1,0:T(8,128)(2,1)S(1)}, bf16[8,128,128]{2,1,0:T(8,128)(2,1)S(1)}, u32[]{:S(2)}, u32[]{:S(2)}) collective-permute-start(bf16[8,128,128]{2,1,0:T(8,128)(2,1)S(1)} %get-tuple-element.112.refs_0_), channel_id=1, source_target_pairs={{0,6},{2,0},{4,2},{6,4},{1,7},{3,1},{5,3},{7,5},{8,14},{10,8},{12,... | collective-permute-start | bytes 786440 | tf_op jit(solution)/shard_map/ppermute | solution.py:387
  26.0 2.7 %collective-permute-done.6.refs_4_ = bf16[8,128,128]{2,1,0:T(8,128)(2,1)S(1)} collective-permute-done((bf16[8,128,128]{2,1,0:T(8,128)(2,1)S(1)}, bf16[8,128,128]{2,1,0:T(8,128)(2,1)S(1)}, u32[]{:S(2)}, u32[]{:S(2)}) %collective-permute-start.6) | collective-permute-done | bytes 262176 | tf_op jit(solution)/shard_map/ppermute | solution.py:387
  28.7 3.5 %collective-permute-start.7 = (bf16[4,128,128]{2,1,0:T(8,128)(2,1)S(1)}, bf16[4,128,128]{2,1,0:T(8,128)(2,1)S(1)}, u32[]{:S(2)}, u32[]{:S(2)}) collective-permute-start(bf16[4,128,128]{2,1,0:T(8,128)(2,1)S(1)} %slice.49), channel_id=1, source_target_pairs={{0,6},{2,0},{4,2},{6,4},{1,7},{3,1},{5,3},{7,5},{8,14},{10,8},{12,... | collective-permute-start | bytes 393224 | tf_op jit(solution)/shard_map/ppermute | solution.py:387
  37.3 2.7 %collective-permute-done.9.refs_7_ = bf16[4,128,128]{2,1,0:T(8,128)(2,1)S(1)} collective-permute-done((bf16[4,128,128]{2,1,0:T(8,128)(2,1)S(1)}, bf16[4,128,128]{2,1,0:T(8,128)(2,1)S(1)}, u32[]{:S(2)}, u32[]{:S(2)}) %collective-permute-start.9) | collective-permute-done | bytes 131104 | tf_op jit(solution)/shard_map/ppermute | solution.py:387
  44.9 17.5 %collective-permute-done.14.w4.refs_14_ = bf16[32,128,128]{2,1,0:T(8,128)(2,1)S(1)} collective-permute-done((bf16[32,128,128]{2,1,0:T(8,128)(2,1)S(1)}, bf16[32,128,128]{2,1,0:T(8,128)(2,1)S(1)}, u32[]{:S(2)}, u32[]{:S(2)}) %collective-permute-start.14) | collective-permute-done | bytes 1048608 | tf_op jit(solution)/shard_map/ppermute | solution.py:387
  64.1 2.8 %collective-permute-start.20 = (bf16[17,128,128]{2,1,0:T(8,128)(2,1)S(1)}, bf16[17,128,128]{2,1,0:T(8,128)(2,1)S(1)}, u32[]{:S(2)}, u32[]{:S(2)}) collective-permute-start(bf16[17,128,128]{2,1,0:T(8,128)(2,1)S(1)} %slice.55), channel_id=1, source_target_pairs={{0,6},{2,0},{4,2},{6,4},{1,7},{3,1},{5,3},{7,5},{8,14},{10,8},{12,... | collective-permute-start | bytes 1671176 | tf_op jit(solution)/shard_map/ppermute | solution.py:387
  69.1 4.3 %collective-permute-done.15.w3.refs_13_ = bf16[17,128,128]{2,1,0:T(8,128)(2,1)S(1)} collective-permute-done((bf16[17,128,128]{2,1,0:T(8,128)(2,1)S(1)}, bf16[17,128,128]{2,1,0:T(8,128)(2,1)S(1)}, u32[]{:S(2)}, u32[]{:S(2)}) %collective-permute-start.15) | collective-permute-done | bytes 557088 | tf_op jit(solution)/shard_map/ppermute | solution.py:387
  76.6 5.0 %collective-permute-start.16 = (bf16[2064,128]{1,0:T(8,128)(2,1)S(1)}, bf16[2064,128]{1,0:T(8,128)(2,1)S(1)}, u32[]{:S(2)}, u32[]{:S(2)}) collective-permute-start(bf16[2064,128]{1,0:T(8,128)(2,1)S(1)} %get-tuple-element.116), channel_id=1, source_target_pairs={{0,32},{32,0},{1,33},{33,1},{2,34},{34,2},{3,35},{35,3},{4,36},{36... | collective-permute-start | bytes 1585160 | tf_op jit(solution)/shard_map/ppermute | solution.py:383
  83.1 2.7 %shard_map.81 = (bf16[4096,128]{1,0:T(8,128)(2,1)S(1)}, bf16[4096,128]{1,0:T(8,128)(2,1)S(1)}, bf16[4096,128]{1,0:T(8,128)(2,1)S(1)}, f32[8,128]{1,0:T(8,128)S(1...) custom-call(s32[5]{0:T(128)S(1)} %stack.32.place_ref.refs_0_.refs_4_.refs_8_, ...), custom_call_target="tpu_custom_call" | custom-call | tf_op jit(solution)/shard_map/pallas_call | solution.py:372
  88.1 2.7 %shard_map.82 = (bf16[4096,128]{1,0:T(8,128)(2,1)S(1)}, bf16[4096,128]{1,0:T(8,128)(2,1)S(1)}, bf16[4096,128]{1,0:T(8,128)(2,1)S(1)}, f32[8,128]{1,0:T(8,128)S(1...) custom-call(s32[5]{0:T(128)S(1)} %stack.32.place_ref.refs_0_.refs_4_.refs_8_, ...), custom_call_target="tpu_custom_call" | custom-call | tf_op jit(solution)/shard_map/pallas_call | solution.py:372
  92.8 2.7 %shard_map.83 = (bf16[4096,128]{1,0:T(8,128)(2,1)S(1)}, bf16[4096,128]{1,0:T(8,128)(2,1)S(1)}, bf16[4096,128]{1,0:T(8,128)(2,1)S(1)}, f32[8,128]{1,0:T(8,128)S(1...) custom-call(s32[5]{0:T(128)S(1)} %stack.32.place_ref.refs_0_.refs_4_.refs_8_, ...), custom_call_target="tpu_custom_call" | custom-call | tf_op jit(solution)/shard_map/pallas_call | solution.py:372
  112.2 9.7 %collective-permute-start.27 = (bf16[2064,128]{1,0:T(8,128)(2,1)S(1)}, bf16[2064,128]{1,0:T(8,128)(2,1)S(1)}, u32[]{:S(2)}, u32[]{:S(2)}) collective-permute-start(bf16[2064,128]{1,0:T(8,128)(2,1)S(1)} %get-tuple-element.183), channel_id=1, source_target_pairs={{0,32},{32,0},{1,33},{33,1},{2,34},{34,2},{3,35},{35,3},{4,36},{36... | collective-permute-start | bytes 1585160 | tf_op jit(solution)/shard_map/ppermute | solution.py:383
  129.9 2.7 %collective-permute-start.32 = (bf16[16,128,128]{2,1,0:T(8,128)(2,1)S(1)}, bf16[16,128,128]{2,1,0:T(8,128)(2,1)S(1)}, u32[]{:S(2)}, u32[]{:S(2)}) collective-permute-start(bf16[16,128,128]{2,1,0:T(8,128)(2,1)S(1)} %get-tuple-element.214), channel_id=1, source_target_pairs={{0,6},{2,0},{4,2},{6,4},{1,7},{3,1},{5,3},{7,5},{8,14},{10,8},{12,... | collective-permute-start | bytes 1572872 | tf_op jit(solution)/shard_map/ppermute | solution.py:387
  134.1 2.7 %collective-permute-start.28 = (bf16[16,128,128]{2,1,0:T(8,128)(2,1)S(1)}, bf16[16,128,128]{2,1,0:T(8,128)(2,1)S(1)}, u32[]{:S(2)}, u32[]{:S(2)}) collective-permute-start(bf16[16,128,128]{2,1,0:T(8,128)(2,1)S(1)} %get-tuple-element.216), channel_id=1, source_target_pairs={{0,24},{8,0},{16,8},{24,16},{1,25},{9,1},{17,9},{25,17},{2,26},{10... | collective-permute-start | bytes 1572872 | tf_op jit(solution)/shard_map/ppermute | solution.py:387
  136.8 7.6 %collective-permute-done.33.hi_ref = bf16[16,128,128]{2,1,0:T(8,128)(2,1)S(1)} collective-permute-done((bf16[16,128,128]{2,1,0:T(8,128)(2,1)S(1)}, bf16[16,128,128]{2,1,0:T(8,128)(2,1)S(1)}, u32[]{:S(2)}, u32[]{:S(2)}) %collective-permute-start.33) | collective-permute-done | bytes 524320 | tf_op jit(solution)/shard_map/ppermute | solution.py:387
  151.3 17.7 %collective-permute-done.34.refs_4_ = bf16[32,128,128]{2,1,0:T(8,128)(2,1)S(1)} collective-permute-done((bf16[32,128,128]{2,1,0:T(8,128)(2,1)S(1)}, bf16[32,128,128]{2,1,0:T(8,128)(2,1)S(1)}, u32[]{:S(2)}, u32[]{:S(2)}) %collective-permute-start.34) | collective-permute-done | bytes 1048608 | tf_op jit(solution)/shard_map/ppermute | solution.py:387
  169.0 3.0 %collective-permute-done.35.refs_5_ = bf16[32,128,128]{2,1,0:T(8,128)(2,1)S(1)} collective-permute-done((bf16[32,128,128]{2,1,0:T(8,128)(2,1)S(1)}, bf16[32,128,128]{2,1,0:T(8,128)(2,1)S(1)}, u32[]{:S(2)}, u32[]{:S(2)}) %collective-permute-start.35) | collective-permute-done | bytes 1048608 | tf_op jit(solution)/shard_map/ppermute | solution.py:387
  172.0 3.0 %collective-permute-done.31.refs_2_ = bf16[32,128,128]{2,1,0:T(8,128)(2,1)S(1)} collective-permute-done((bf16[32,128,128]{2,1,0:T(8,128)(2,1)S(1)}, bf16[32,128,128]{2,1,0:T(8,128)(2,1)S(1)}, u32[]{:S(2)}, u32[]{:S(2)}) %collective-permute-start.31) | collective-permute-done | bytes 1048608 | tf_op jit(solution)/shard_map/ppermute | solution.py:387
  179.9 3.8 %collective-permute-done.36.refs_1_ = bf16[2,4,128,128]{3,2,1,0:T(8,128)(2,1)S(1)} collective-permute-done((bf16[2,4,128,128]{3,2,1,0:T(8,128)(2,1)S(1)}, bf16[2,4,128,128]{3,2,1,0:T(8,128)(2,1)S(1)}, u32[]{:S(2)}, u32[]{:S(2)}) %collective-permute-start.36) | collective-permute-done | bytes 262176 | tf_op jit(solution)/shard_map/ppermute | solution.py:387
  185.2 7.3 %collective-permute-done.38.refs_3_ = bf16[2,4,128,128]{3,2,1,0:T(8,128)(2,1)S(1)} collective-permute-done((bf16[2,4,128,128]{3,2,1,0:T(8,128)(2,1)S(1)}, bf16[2,4,128,128]{3,2,1,0:T(8,128)(2,1)S(1)}, u32[]{:S(2)}, u32[]{:S(2)}) %collective-permute-start.38) | collective-permute-done | bytes 262176 | tf_op jit(solution)/shard_map/ppermute | solution.py:387
  201.6 6.1 %collective-permute-start.45 = (f32[2,128,128]{2,1,0:T(8,128)S(1)}, f32[2,128,128]{2,1,0:T(8,128)S(1)}, u32[]{:S(2)}, u32[]{:S(2)}) collective-permute-start(f32[2,128,128]{2,1,0:T(8,128)S(1)} %get-tuple-element.209), channel_id=1, source_target_pairs={{0,32},{32,0},{1,33},{33,1},{2,34},{34,2},{3,35},{35,3},{4,36},{36... | collective-permute-start | bytes 393224 | tf_op jit(solution)/shard_map/ppermute | solution.py:383
  (117 shorter events, 85.4 us)
Async XLA Ops:
  9.7 9.4 %collective-permute-start.1 = (bf16[2,2,128,128]{3,2,1,0:T(8,128)(2,1)S(1)}, bf16[2,2,128,128]{3,2,1,0:T(8,128)(2,1)S(1)}, u32[]{:S(2)}, u32[]{:S(2)}) collective-permute-start(bf16[2,2,128,128]{3,2,1,0:T(8,128)(2,1)S(1)} %pad_maximum_fusion.p0), channel_id=1, source_target_pairs={{0,1},{1,64},{64,65},{65,0},{2,3},{3,66},{66,67},{67,2},{4,5},{5,6... | collective-permute-start | bytes 393224 | tf_op jit(solution)/shard_map/ppermute | solution.py:387
  19.7 9.0 %collective-permute-start.6 = (bf16[8,128,128]{2,1,0:T(8,128)(2,1)S(1)}, bf16[8,128,128]{2,1,0:T(8,128)(2,1)S(1)}, u32[]{:S(2)}, u32[]{:S(2)}) collective-permute-start(bf16[8,128,128]{2,1,0:T(8,128)(2,1)S(1)} %get-tuple-element.112.refs_0_), channel_id=1, source_target_pairs={{0,6},{2,0},{4,2},{6,4},{1,7},{3,1},{5,3},{7,5},{8,14},{10,8},{12,... | collective-permute-start | bytes 786440 | tf_op jit(solution)/shard_map/ppermute | solution.py:387
  26.0 8.9 %collective-permute-start.8 = (bf16[8,128,128]{2,1,0:T(8,128)(2,1)S(1)}, bf16[8,128,128]{2,1,0:T(8,128)(2,1)S(1)}, u32[]{:S(2)}, u32[]{:S(2)}) collective-permute-start(bf16[8,128,128]{2,1,0:T(8,128)(2,1)S(1)} %get-tuple-element.113.refs_5_), channel_id=1, source_target_pairs={{0,8},{8,16},{16,24},{24,0},{1,9},{9,17},{17,25},{25,1},{2,10},{10... | collective-permute-start | bytes 786440 | tf_op jit(solution)/shard_map/ppermute | solution.py:387
  40.7 21.7 %collective-permute-start.14 = (bf16[32,128,128]{2,1,0:T(8,128)(2,1)S(1)}, bf16[32,128,128]{2,1,0:T(8,128)(2,1)S(1)}, u32[]{:S(2)}, u32[]{:S(2)}) collective-permute-start(bf16[32,128,128]{2,1,0:T(8,128)(2,1)S(1)} %get-tuple-element.114.w0.refs_10_), channel_id=1, source_target_pairs={{0,24},{8,0},{16,8},{24,16},{1,25},{9,1},{17,9},{25,17},{2,26},{10... | collective-permute-start | bytes 3145736 | tf_op jit(solution)/shard_map/ppermute | solution.py:387
  40.8 23.2 %collective-permute-start.12 = (bf16[32,128,128]{2,1,0:T(8,128)(2,1)S(1)}, bf16[32,128,128]{2,1,0:T(8,128)(2,1)S(1)}, u32[]{:S(2)}, u32[]{:S(2)}) collective-permute-start(bf16[32,128,128]{2,1,0:T(8,128)(2,1)S(1)} %get-tuple-element.114.w0.refs_10_), channel_id=1, source_target_pairs={{0,8},{8,16},{16,24},{24,0},{1,9},{9,17},{17,25},{25,1},{2,10},{10... | collective-permute-start | bytes 3145736 | tf_op jit(solution)/shard_map/ppermute | solution.py:387
  42.2 21.9 %collective-permute-start.19 = (bf16[32,128,128]{2,1,0:T(8,128)(2,1)S(1)}, bf16[32,128,128]{2,1,0:T(8,128)(2,1)S(1)}, u32[]{:S(2)}, u32[]{:S(2)}) collective-permute-start(bf16[32,128,128]{2,1,0:T(8,128)(2,1)S(1)} %get-tuple-element.118.l0.refs_15_), channel_id=1, source_target_pairs={{0,6},{2,0},{4,2},{6,4},{1,7},{3,1},{5,3},{7,5},{8,14},{10,8},{12,... | collective-permute-start | bytes 3145736 | tf_op jit(solution)/shard_map/ppermute | solution.py:387
  44.9 22.1 %collective-permute-start.17 = (bf16[32,128,128]{2,1,0:T(8,128)(2,1)S(1)}, bf16[32,128,128]{2,1,0:T(8,128)(2,1)S(1)}, u32[]{:S(2)}, u32[]{:S(2)}) collective-permute-start(bf16[32,128,128]{2,1,0:T(8,128)(2,1)S(1)} %get-tuple-element.118.l0.refs_15_), channel_id=1, source_target_pairs={{0,2},{2,4},{4,6},{6,0},{1,3},{3,5},{5,7},{7,1},{8,10},{10,12},{12... | collective-permute-start | bytes 3145736 | tf_op jit(solution)/shard_map/ppermute | solution.py:387
  62.4 11.0 %collective-permute-start.15 = (bf16[17,128,128]{2,1,0:T(8,128)(2,1)S(1)}, bf16[17,128,128]{2,1,0:T(8,128)(2,1)S(1)}, u32[]{:S(2)}, u32[]{:S(2)}) collective-permute-start(bf16[17,128,128]{2,1,0:T(8,128)(2,1)S(1)} %slice.53), channel_id=1, source_target_pairs={{0,24},{8,0},{16,8},{24,16},{1,25},{9,1},{17,9},{25,17},{2,26},{10... | collective-permute-start | bytes 1671176 | tf_op jit(solution)/shard_map/ppermute | solution.py:387
  64.0 11.4 %collective-permute-start.13 = (bf16[17,128,128]{2,1,0:T(8,128)(2,1)S(1)}, bf16[17,128,128]{2,1,0:T(8,128)(2,1)S(1)}, u32[]{:S(2)}, u32[]{:S(2)}) collective-permute-start(bf16[17,128,128]{2,1,0:T(8,128)(2,1)S(1)} %slice.52), channel_id=1, source_target_pairs={{0,8},{8,16},{16,24},{24,0},{1,9},{9,17},{17,25},{25,1},{2,10},{10... | collective-permute-start | bytes 1671176 | tf_op jit(solution)/shard_map/ppermute | solution.py:387
  64.1 17.4 %collective-permute-start.20 = (bf16[17,128,128]{2,1,0:T(8,128)(2,1)S(1)}, bf16[17,128,128]{2,1,0:T(8,128)(2,1)S(1)}, u32[]{:S(2)}, u32[]{:S(2)}) collective-permute-start(bf16[17,128,128]{2,1,0:T(8,128)(2,1)S(1)} %slice.55), channel_id=1, source_target_pairs={{0,6},{2,0},{4,2},{6,4},{1,7},{3,1},{5,3},{7,5},{8,14},{10,8},{12,... | collective-permute-start | bytes 1671176 | tf_op jit(solution)/shard_map/ppermute | solution.py:387
  67.0 14.6 %collective-permute-start.18 = (bf16[17,128,128]{2,1,0:T(8,128)(2,1)S(1)}, bf16[17,128,128]{2,1,0:T(8,128)(2,1)S(1)}, u32[]{:S(2)}, u32[]{:S(2)}) collective-permute-start(bf16[17,128,128]{2,1,0:T(8,128)(2,1)S(1)} %slice.54), channel_id=1, source_target_pairs={{0,2},{2,4},{4,6},{6,0},{1,3},{3,5},{5,7},{7,1},{8,10},{10,12},{12... | collective-permute-start | bytes 1671176 | tf_op jit(solution)/shard_map/ppermute | solution.py:387
  112.2 20.4 %collective-permute-start.27 = (bf16[2064,128]{1,0:T(8,128)(2,1)S(1)}, bf16[2064,128]{1,0:T(8,128)(2,1)S(1)}, u32[]{:S(2)}, u32[]{:S(2)}) collective-permute-start(bf16[2064,128]{1,0:T(8,128)(2,1)S(1)} %get-tuple-element.183), channel_id=1, source_target_pairs={{0,32},{32,0},{1,33},{33,1},{2,34},{34,2},{3,35},{35,3},{4,36},{36... | collective-permute-start | bytes 1585160 | tf_op jit(solution)/shard_map/ppermute | solution.py:383
  129.8 14.7 %collective-permute-start.33 = (bf16[16,128,128]{2,1,0:T(8,128)(2,1)S(1)}, bf16[16,128,128]{2,1,0:T(8,128)(2,1)S(1)}, u32[]{:S(2)}, u32[]{:S(2)}) collective-permute-start(bf16[16,128,128]{2,1,0:T(8,128)(2,1)S(1)} %get-tuple-element.213), channel_id=1, source_target_pairs={{0,2},{2,4},{4,6},{6,0},{1,3},{3,5},{5,7},{7,1},{8,10},{10,12},{12... | collective-permute-start | bytes 1572872 | tf_op jit(solution)/shard_map/ppermute | solution.py:387
  129.9 14.6 %collective-permute-start.32 = (bf16[16,128,128]{2,1,0:T(8,128)(2,1)S(1)}, bf16[16,128,128]{2,1,0:T(8,128)(2,1)S(1)}, u32[]{:S(2)}, u32[]{:S(2)}) collective-permute-start(bf16[16,128,128]{2,1,0:T(8,128)(2,1)S(1)} %get-tuple-element.214), channel_id=1, source_target_pairs={{0,6},{2,0},{4,2},{6,4},{1,7},{3,1},{5,3},{7,5},{8,14},{10,8},{12,... | collective-permute-start | bytes 1572872 | tf_op jit(solution)/shard_map/ppermute | solution.py:387
  134.0 14.0 %collective-permute-start.29 = (bf16[16,128,128]{2,1,0:T(8,128)(2,1)S(1)}, bf16[16,128,128]{2,1,0:T(8,128)(2,1)S(1)}, u32[]{:S(2)}, u32[]{:S(2)}) collective-permute-start(bf16[16,128,128]{2,1,0:T(8,128)(2,1)S(1)} %get-tuple-element.215), channel_id=1, source_target_pairs={{0,8},{8,16},{16,24},{24,0},{1,9},{9,17},{17,25},{25,1},{2,10},{10... | collective-permute-start | bytes 1572872 | tf_op jit(solution)/shard_map/ppermute | solution.py:387
  134.1 13.9 %collective-permute-start.28 = (bf16[16,128,128]{2,1,0:T(8,128)(2,1)S(1)}, bf16[16,128,128]{2,1,0:T(8,128)(2,1)S(1)}, u32[]{:S(2)}, u32[]{:S(2)}) collective-permute-start(bf16[16,128,128]{2,1,0:T(8,128)(2,1)S(1)} %get-tuple-element.216), channel_id=1, source_target_pairs={{0,24},{8,0},{16,8},{24,16},{1,25},{9,1},{17,9},{25,17},{2,26},{10... | collective-permute-start | bytes 1572872 | tf_op jit(solution)/shard_map/ppermute | solution.py:387
  145.2 23.8 %collective-permute-start.34 = (bf16[32,128,128]{2,1,0:T(8,128)(2,1)S(1)}, bf16[32,128,128]{2,1,0:T(8,128)(2,1)S(1)}, u32[]{:S(2)}, u32[]{:S(2)}) collective-permute-start(bf16[32,128,128]{2,1,0:T(8,128)(2,1)S(1)} %get-tuple-element.194), channel_id=1, source_target_pairs={{0,6},{2,0},{4,2},{6,4},{1,7},{3,1},{5,3},{7,5},{8,14},{10,8},{12,... | collective-permute-start | bytes 3145736 | tf_op jit(solution)/shard_map/ppermute | solution.py:387
  147.7 24.3 %collective-permute-start.35 = (bf16[32,128,128]{2,1,0:T(8,128)(2,1)S(1)}, bf16[32,128,128]{2,1,0:T(8,128)(2,1)S(1)}, u32[]{:S(2)}, u32[]{:S(2)}) collective-permute-start(bf16[32,128,128]{2,1,0:T(8,128)(2,1)S(1)} %get-tuple-element.195), channel_id=1, source_target_pairs={{0,2},{2,4},{4,6},{6,0},{1,3},{3,5},{5,7},{7,1},{8,10},{10,12},{12... | collective-permute-start | bytes 3145736 | tf_op jit(solution)/shard_map/ppermute | solution.py:387
  148.9 23.1 %collective-permute-start.30 = (bf16[32,128,128]{2,1,0:T(8,128)(2,1)S(1)}, bf16[32,128,128]{2,1,0:T(8,128)(2,1)S(1)}, u32[]{:S(2)}, u32[]{:S(2)}) collective-permute-start(bf16[32,128,128]{2,1,0:T(8,128)(2,1)S(1)} %get-tuple-element.188), channel_id=1, source_target_pairs={{0,24},{8,0},{16,8},{24,16},{1,25},{9,1},{17,9},{25,17},{2,26},{10... | collective-permute-start | bytes 3145736 | tf_op jit(solution)/shard_map/ppermute | solution.py:387
  151.3 23.7 %collective-permute-start.31 = (bf16[32,128,128]{2,1,0:T(8,128)(2,1)S(1)}, bf16[32,128,128]{2,1,0:T(8,128)(2,1)S(1)}, u32[]{:S(2)}, u32[]{:S(2)}) collective-permute-start(bf16[32,128,128]{2,1,0:T(8,128)(2,1)S(1)} %get-tuple-element.189), channel_id=1, source_target_pairs={{0,8},{8,16},{16,24},{24,0},{1,9},{9,17},{17,25},{25,1},{2,10},{10... | collective-permute-start | bytes 3145736 | tf_op jit(solution)/shard_map/ppermute | solution.py:387
  178.4 14.1 %collective-permute-start.38 = (bf16[2,4,128,128]{3,2,1,0:T(8,128)(2,1)S(1)}, bf16[2,4,128,128]{3,2,1,0:T(8,128)(2,1)S(1)}, u32[]{:S(2)}, u32[]{:S(2)}) collective-permute-start(bf16[2,4,128,128]{3,2,1,0:T(8,128)(2,1)S(1)} %get-tuple-element.199), channel_id=1, source_target_pairs={{0,2},{2,4},{4,6},{6,0},{1,3},{3,5},{5,7},{7,1},{8,10},{10,12},{12... | collective-permute-start | bytes 786440 | tf_op jit(solution)/shard_map/ppermute | solution.py:387
  179.0 13.5 %collective-permute-start.39 = (bf16[2,4,128,128]{3,2,1,0:T(8,128)(2,1)S(1)}, bf16[2,4,128,128]{3,2,1,0:T(8,128)(2,1)S(1)}, u32[]{:S(2)}, u32[]{:S(2)}) collective-permute-start(bf16[2,4,128,128]{3,2,1,0:T(8,128)(2,1)S(1)} %get-tuple-element.201), channel_id=1, source_target_pairs={{0,24},{8,0},{16,8},{24,16},{1,25},{9,1},{17,9},{25,17},{2,26},{10... | collective-permute-start | bytes 786440 | tf_op jit(solution)/shard_map/ppermute | solution.py:387
  179.3 13.2 %collective-permute-start.40 = (bf16[2,4,128,128]{3,2,1,0:T(8,128)(2,1)S(1)}, bf16[2,4,128,128]{3,2,1,0:T(8,128)(2,1)S(1)}, u32[]{:S(2)}, u32[]{:S(2)}) collective-permute-start(bf16[2,4,128,128]{3,2,1,0:T(8,128)(2,1)S(1)} %get-tuple-element.202), channel_id=1, source_target_pairs={{0,16},{8,24},{16,0},{24,8},{1,17},{9,25},{17,1},{25,9},{2,18},{10... | collective-permute-start | bytes 786440 | tf_op jit(solution)/shard_map/ppermute | solution.py:387
  183.7 9.5 %collective-permute-start.41 = (bf16[2,4,128,128]{3,2,1,0:T(8,128)(2,1)S(1)}, bf16[2,4,128,128]{3,2,1,0:T(8,128)(2,1)S(1)}, u32[]{:S(2)}, u32[]{:S(2)}) collective-permute-start(bf16[2,4,128,128]{3,2,1,0:T(8,128)(2,1)S(1)} %get-tuple-element.203), channel_id=1, source_target_pairs={{0,8},{8,16},{16,24},{24,0},{1,9},{9,17},{17,25},{25,1},{2,10},{10... | collective-permute-start | bytes 786440 | tf_op jit(solution)/shard_map/ppermute | solution.py:387
  (29 other events, 302.7 us)
where the time goes:
time: 215 us; the launch traced here: 211 us
  waiting for transfers between devices  103 us (48%)
  starting transfers between devices  65.9 us (31%)
  Pallas kernels  37.8 us (18%)
  local copies, waits for them, and re-layouts  2.85 us (1%)
    ppermute x36, waiting for transfers between devices, ring(): return lax.ppermute(value, axes, [(i, (i + steps) % 4) for i in range(4)])  90.7 us
    ppermute x36, starting transfers between devices, ring(): return lax.ppermute(value, axes, [(i, (i + steps) % 4) for i in range(4)])  40.6 us
    pallas_call x17, Pallas kernels, call(): pl.pallas_call(kernel, out_shape=outs, in_specs=[WHOLE] * len(old) + [SCA...  26.5 us
    ppermute x10, starting transfers between devices, swapped(): return lax.ppermute(value, 'c', SWAP)  25.3 us
    ppermute x10, waiting for transfers between devices, swapped(): return lax.ppermute(value, 'c', SWAP)  12.7 us
    pallas_call x5, Pallas kernels, call_into(): pl.pallas_call(kernel, out_shape=outs, in_specs=[WHOLE] * len(old) + [SCA...  9.26 us
  transfers between devices with their start and end apart: 46, of which 30 were waited for; matrix products, arithmetic and copies ran while one was open for 0% of the time, Pallas kernels for 7%

commit v1 on v0

--- a/solution.py
+++ b/solution.py
@@ -419,7 +419,13 @@
     left = left_factor[0]
     gain = norm_gain.reshape(2, 1, BS)
 
-    keep, send = call(prep_kernel, place, (right, left, gain), (kept(2, BS, BS),) * 2)
+    keep, send = pl.pallas_call(
+        prep_kernel,
+        out_shape=(kept(2, BS, BS),) * 2,
+        in_specs=[SCALARS] + [WHOLE] * 3,
+        out_specs=(WHOLE,) * 2,
+        compiler_params=pltpu.CompilerParams(vmem_limit_bytes=VMEM_LIMIT),
+    )(place, right, left, gain)
     mine = jnp.stack([keep, swapped(send)])
     stage = kept(2, 4, BS, BS)
     part = kept(8, BS, BS)
@@ -475,6 +481,7 @@
     for layer in (3, 2, 1):
         below = layer - 1
         go, gr = uo, swapped(us)
+        go, slabs["left"] = lax.optimization_barrier((go, slabs["left"]))
         pre, uo, us, st, *grad = call(
             functools.partial(backward_kernel, layer), place,
             (go, gr, st, rmss[layer], rmss[below], xs[layer], *([grad] if layer == 3 else grad), slopes[below], perms[below],

time: 215 us -> 210 us (0.977)
  waiting for transfers between devices: 103 us -> 98.9 us
    ppermute x10, waiting for transfers between devices: 12.7 us -> 8.21 us  [swapped(): return lax.ppermute(value, 'c', SWAP)]
    pallas_call x17 -> x16, Pallas kernels: 26.5 us -> 25.7 us  [call(): pl.pallas_call(kernel, out_shape=outs, in_specs=[WHOLE] * len(old) + [SCA...]
  transfers between devices with their start and end apart: 46 -> 46, of which waited for: 30 -> 28; matrix products, arithmetic and copies ran while one was open for 0% -> 0% of each run, Pallas kernels for 7% -> 7%
where the time goes in v1:
time: 210 us; the launch traced here: 207 us
  waiting for transfers between devices  98.9 us (47%)
  starting transfers between devices  65.9 us (31%)
  Pallas kernels  37.9 us (18%)
  local copies, waits for them, and re-layouts  2.8 us (1%)
    ppermute x36, waiting for transfers between devices, ring(): return lax.ppermute(value, axes, [(i, (i + steps) % 4) for i in range(4)])  90.7 us
    ppermute x36, starting transfers between devices, ring(): return lax.ppermute(value, axes, [(i, (i + steps) % 4) for i in range(4)])  40.7 us
    pallas_call x16, Pallas kernels, call(): pl.pallas_call(kernel, out_shape=outs, in_specs=[WHOLE] * len(old) + [SCA...  25.7 us
    ppermute x10, starting transfers between devices, swapped(): return lax.ppermute(value, 'c', SWAP)  25.2 us
    pallas_call x5, Pallas kernels, call_into(): pl.pallas_call(kernel, out_shape=outs, in_specs=[WHOLE] * len(old) + [SCA...  9.22 us
    ppermute x10, waiting for transfers between devices, swapped(): return lax.ppermute(value, 'c', SWAP)  8.21 us
  transfers between devices with their start and end apart: 46, of which 28 were waited for; matrix products, arithmetic and copies ran while one was open for 0% of the time, Pallas kernels for 7%

profile of v1, /device:TPU:1, one launch (start us, length us, event | category | flops | bytes accessed | tf_op | source)
XLA Modules:
  0.0 206.7 jit_solution(6207942032810575316)
XLA Ops:
  6.5 2.9 %collective-permute-start.3 = (bf16[2,2,128,128]{3,2,1,0:T(8,128)(2,1)S(1)}, bf16[2,2,128,128]{3,2,1,0:T(8,128)(2,1)S(1)}, u32[]{:S(2)}, u32[]{:S(2)}) collective-permute-start(bf16[2,2,128,128]{3,2,1,0:T(8,128)(2,1)S(1)} %pad_maximum_fusion.p0), channel_id=1, source_target_pairs={{0,65},{1,0},{64,1},{65,64},{2,67},{3,2},{66,3},{67,66},{4,69},{5,... | collective-permute-start | bytes 393224 | tf_op jit(solution)/shard_map/ppermute | solution.py:387
  10.4 4.2 %collective-permute-done.3.p3 = bf16[2,2,128,128]{3,2,1,0:T(8,128)(2,1)S(1)} collective-permute-done((bf16[2,2,128,128]{3,2,1,0:T(8,128)(2,1)S(1)}, bf16[2,2,128,128]{3,2,1,0:T(8,128)(2,1)S(1)}, u32[]{:S(2)}, u32[]{:S(2)}) %collective-permute-start.3) | collective-permute-done | bytes 131104 | tf_op jit(solution)/shard_map/ppermute | solution.py:387
  15.3 3.8 %collective-permute-done.1.p1 = bf16[2,2,128,128]{3,2,1,0:T(8,128)(2,1)S(1)} collective-permute-done((bf16[2,2,128,128]{3,2,1,0:T(8,128)(2,1)S(1)}, bf16[2,2,128,128]{3,2,1,0:T(8,128)(2,1)S(1)}, u32[]{:S(2)}, u32[]{:S(2)}) %collective-permute-start.1) | collective-permute-done | bytes 131104 | tf_op jit(solution)/shard_map/ppermute | solution.py:387
  19.7 3.8 %collective-permute-start.6 = (bf16[8,128,128]{2,1,0:T(8,128)(2,1)S(1)}, bf16[8,128,128]{2,1,0:T(8,128)(2,1)S(1)}, u32[]{:S(2)}, u32[]{:S(2)}) collective-permute-start(bf16[8,128,128]{2,1,0:T(8,128)(2,1)S(1)} %get-tuple-element.127.refs_0_), channel_id=1, source_target_pairs={{0,6},{2,0},{4,2},{6,4},{1,7},{3,1},{5,3},{7,5},{8,14},{10,8},{12,... | collective-permute-start | bytes 786440 | tf_op jit(solution)/shard_map/ppermute | solution.py:387
  26.0 2.7 %collective-permute-done.6.refs_4_ = bf16[8,128,128]{2,1,0:T(8,128)(2,1)S(1)} collective-permute-done((bf16[8,128,128]{2,1,0:T(8,128)(2,1)S(1)}, bf16[8,128,128]{2,1,0:T(8,128)(2,1)S(1)}, u32[]{:S(2)}, u32[]{:S(2)}) %collective-permute-start.6) | collective-permute-done | bytes 262176 | tf_op jit(solution)/shard_map/ppermute | solution.py:387
  28.7 3.5 %collective-permute-start.7 = (bf16[4,128,128]{2,1,0:T(8,128)(2,1)S(1)}, bf16[4,128,128]{2,1,0:T(8,128)(2,1)S(1)}, u32[]{:S(2)}, u32[]{:S(2)}) collective-permute-start(bf16[4,128,128]{2,1,0:T(8,128)(2,1)S(1)} %slice.49), channel_id=1, source_target_pairs={{0,6},{2,0},{4,2},{6,4},{1,7},{3,1},{5,3},{7,5},{8,14},{10,8},{12,... | collective-permute-start | bytes 393224 | tf_op jit(solution)/shard_map/ppermute | solution.py:387
  37.3 2.7 %collective-permute-done.9.refs_7_ = bf16[4,128,128]{2,1,0:T(8,128)(2,1)S(1)} collective-permute-done((bf16[4,128,128]{2,1,0:T(8,128)(2,1)S(1)}, bf16[4,128,128]{2,1,0:T(8,128)(2,1)S(1)}, u32[]{:S(2)}, u32[]{:S(2)}) %collective-permute-start.9) | collective-permute-done | bytes 131104 | tf_op jit(solution)/shard_map/ppermute | solution.py:387
  44.9 17.5 %collective-permute-done.14.w4.refs_14_ = bf16[32,128,128]{2,1,0:T(8,128)(2,1)S(1)} collective-permute-done((bf16[32,128,128]{2,1,0:T(8,128)(2,1)S(1)}, bf16[32,128,128]{2,1,0:T(8,128)(2,1)S(1)}, u32[]{:S(2)}, u32[]{:S(2)}) %collective-permute-start.14) | collective-permute-done | bytes 1048608 | tf_op jit(solution)/shard_map/ppermute | solution.py:387
  64.1 2.8 %collective-permute-start.20 = (bf16[17,128,128]{2,1,0:T(8,128)(2,1)S(1)}, bf16[17,128,128]{2,1,0:T(8,128)(2,1)S(1)}, u32[]{:S(2)}, u32[]{:S(2)}) collective-permute-start(bf16[17,128,128]{2,1,0:T(8,128)(2,1)S(1)} %slice.55), channel_id=1, source_target_pairs={{0,6},{2,0},{4,2},{6,4},{1,7},{3,1},{5,3},{7,5},{8,14},{10,8},{12,... | collective-permute-start | bytes 1671176 | tf_op jit(solution)/shard_map/ppermute | solution.py:387
  69.1 4.3 %collective-permute-done.15.w3.refs_13_ = bf16[17,128,128]{2,1,0:T(8,128)(2,1)S(1)} collective-permute-done((bf16[17,128,128]{2,1,0:T(8,128)(2,1)S(1)}, bf16[17,128,128]{2,1,0:T(8,128)(2,1)S(1)}, u32[]{:S(2)}, u32[]{:S(2)}) %collective-permute-start.15) | collective-permute-done | bytes 557088 | tf_op jit(solution)/shard_map/ppermute | solution.py:387
  76.6 5.0 %collective-permute-start.16 = (bf16[2064,128]{1,0:T(8,128)(2,1)S(1)}, bf16[2064,128]{1,0:T(8,128)(2,1)S(1)}, u32[]{:S(2)}, u32[]{:S(2)}) collective-permute-start(bf16[2064,128]{1,0:T(8,128)(2,1)S(1)} %get-tuple-element.131), channel_id=1, source_target_pairs={{0,32},{32,0},{1,33},{33,1},{2,34},{34,2},{3,35},{35,3},{4,36},{36... | collective-permute-start | bytes 1585160 | tf_op jit(solution)/shard_map/ppermute | solution.py:383
  83.1 2.7 %shard_map.81 = (bf16[4096,128]{1,0:T(8,128)(2,1)S(1)}, bf16[4096,128]{1,0:T(8,128)(2,1)S(1)}, bf16[4096,128]{1,0:T(8,128)(2,1)S(1)}, f32[8,128]{1,0:T(8,128)S(1...) custom-call(s32[5]{0:T(128)S(1)} %stack.32.place_ref.refs_0_.refs_4_.refs_8_, ...), custom_call_target="tpu_custom_call" | custom-call | tf_op jit(solution)/shard_map/pallas_call | solution.py:372
  88.1 2.7 %shard_map.82 = (bf16[4096,128]{1,0:T(8,128)(2,1)S(1)}, bf16[4096,128]{1,0:T(8,128)(2,1)S(1)}, bf16[4096,128]{1,0:T(8,128)(2,1)S(1)}, f32[8,128]{1,0:T(8,128)S(1...) custom-call(s32[5]{0:T(128)S(1)} %stack.32.place_ref.refs_0_.refs_4_.refs_8_, ...), custom_call_target="tpu_custom_call" | custom-call | tf_op jit(solution)/shard_map/pallas_call | solution.py:372
  92.8 2.7 %shard_map.83 = (bf16[4096,128]{1,0:T(8,128)(2,1)S(1)}, bf16[4096,128]{1,0:T(8,128)(2,1)S(1)}, bf16[4096,128]{1,0:T(8,128)(2,1)S(1)}, f32[8,128]{1,0:T(8,128)S(1...) custom-call(s32[5]{0:T(128)S(1)} %stack.32.place_ref.refs_0_.refs_4_.refs_8_, ...), custom_call_target="tpu_custom_call" | custom-call | tf_op jit(solution)/shard_map/pallas_call | solution.py:372
  108.4 9.7 %collective-permute-start.26 = (bf16[2064,128]{1,0:T(8,128)(2,1)S(1)}, bf16[2064,128]{1,0:T(8,128)(2,1)S(1)}, u32[]{:S(2)}, u32[]{:S(2)}) collective-permute-start(bf16[2064,128]{1,0:T(8,128)(2,1)S(1)} %get-tuple-element.201), channel_id=1, source_target_pairs={{0,32},{32,0},{1,33},{33,1},{2,34},{34,2},{3,35},{35,3},{4,36},{36... | collective-permute-start | bytes 1585160 | tf_op jit(solution)/shard_map/ppermute | solution.py:383
  125.4 2.7 %collective-permute-start.32 = (bf16[16,128,128]{2,1,0:T(8,128)(2,1)S(1)}, bf16[16,128,128]{2,1,0:T(8,128)(2,1)S(1)}, u32[]{:S(2)}, u32[]{:S(2)}) collective-permute-start(bf16[16,128,128]{2,1,0:T(8,128)(2,1)S(1)} %get-tuple-element.244), channel_id=1, source_target_pairs={{0,6},{2,0},{4,2},{6,4},{1,7},{3,1},{5,3},{7,5},{8,14},{10,8},{12,... | collective-permute-start | bytes 1572872 | tf_op jit(solution)/shard_map/ppermute | solution.py:387
  129.7 2.7 %collective-permute-start.28 = (bf16[16,128,128]{2,1,0:T(8,128)(2,1)S(1)}, bf16[16,128,128]{2,1,0:T(8,128)(2,1)S(1)}, u32[]{:S(2)}, u32[]{:S(2)}) collective-permute-start(bf16[16,128,128]{2,1,0:T(8,128)(2,1)S(1)} %get-tuple-element.246), channel_id=1, source_target_pairs={{0,24},{8,0},{16,8},{24,16},{1,25},{9,1},{17,9},{25,17},{2,26},{10... | collective-permute-start | bytes 1572872 | tf_op jit(solution)/shard_map/ppermute | solution.py:387
  132.3 7.7 %collective-permute-done.33.hi_ref = bf16[16,128,128]{2,1,0:T(8,128)(2,1)S(1)} collective-permute-done((bf16[16,128,128]{2,1,0:T(8,128)(2,1)S(1)}, bf16[16,128,128]{2,1,0:T(8,128)(2,1)S(1)}, u32[]{:S(2)}, u32[]{:S(2)}) %collective-permute-start.33) | collective-permute-done | bytes 524320 | tf_op jit(solution)/shard_map/ppermute | solution.py:387
  146.8 17.7 %collective-permute-done.34.refs_4_ = bf16[32,128,128]{2,1,0:T(8,128)(2,1)S(1)} collective-permute-done((bf16[32,128,128]{2,1,0:T(8,128)(2,1)S(1)}, bf16[32,128,128]{2,1,0:T(8,128)(2,1)S(1)}, u32[]{:S(2)}, u32[]{:S(2)}) %collective-permute-start.34) | collective-permute-done | bytes 1048608 | tf_op jit(solution)/shard_map/ppermute | solution.py:387
  164.6 3.0 %collective-permute-done.35.refs_5_ = bf16[32,128,128]{2,1,0:T(8,128)(2,1)S(1)} collective-permute-done((bf16[32,128,128]{2,1,0:T(8,128)(2,1)S(1)}, bf16[32,128,128]{2,1,0:T(8,128)(2,1)S(1)}, u32[]{:S(2)}, u32[]{:S(2)}) %collective-permute-start.35) | collective-permute-done | bytes 1048608 | tf_op jit(solution)/shard_map/ppermute | solution.py:387
  167.5 3.0 %collective-permute-done.31.refs_2_ = bf16[32,128,128]{2,1,0:T(8,128)(2,1)S(1)} collective-permute-done((bf16[32,128,128]{2,1,0:T(8,128)(2,1)S(1)}, bf16[32,128,128]{2,1,0:T(8,128)(2,1)S(1)}, u32[]{:S(2)}, u32[]{:S(2)}) %collective-permute-start.31) | collective-permute-done | bytes 1048608 | tf_op jit(solution)/shard_map/ppermute | solution.py:387
  175.5 4.0 %collective-permute-done.36.refs_1_ = bf16[2,4,128,128]{3,2,1,0:T(8,128)(2,1)S(1)} collective-permute-done((bf16[2,4,128,128]{3,2,1,0:T(8,128)(2,1)S(1)}, bf16[2,4,128,128]{3,2,1,0:T(8,128)(2,1)S(1)}, u32[]{:S(2)}, u32[]{:S(2)}) %collective-permute-start.36) | collective-permute-done | bytes 262176 | tf_op jit(solution)/shard_map/ppermute | solution.py:387
  180.8 7.3 %collective-permute-done.38.refs_3_ = bf16[2,4,128,128]{3,2,1,0:T(8,128)(2,1)S(1)} collective-permute-done((bf16[2,4,128,128]{3,2,1,0:T(8,128)(2,1)S(1)}, bf16[2,4,128,128]{3,2,1,0:T(8,128)(2,1)S(1)}, u32[]{:S(2)}, u32[]{:S(2)}) %collective-permute-start.38) | collective-permute-done | bytes 262176 | tf_op jit(solution)/shard_map/ppermute | solution.py:387
  197.3 6.0 %collective-permute-start.45 = (f32[2,128,128]{2,1,0:T(8,128)S(1)}, f32[2,128,128]{2,1,0:T(8,128)S(1)}, u32[]{:S(2)}, u32[]{:S(2)}) collective-permute-start(f32[2,128,128]{2,1,0:T(8,128)S(1)} %get-tuple-element.239), channel_id=1, source_target_pairs={{0,32},{32,0},{1,33},{33,1},{2,34},{34,2},{3,35},{35,3},{4,36},{36... | collective-permute-start | bytes 393224 | tf_op jit(solution)/shard_map/ppermute | solution.py:383
  (117 shorter events, 80.8 us)
Async XLA Ops:
  9.7 9.4 %collective-permute-start.1 = (bf16[2,2,128,128]{3,2,1,0:T(8,128)(2,1)S(1)}, bf16[2,2,128,128]{3,2,1,0:T(8,128)(2,1)S(1)}, u32[]{:S(2)}, u32[]{:S(2)}) collective-permute-start(bf16[2,2,128,128]{3,2,1,0:T(8,128)(2,1)S(1)} %pad_maximum_fusion.p0), channel_id=1, source_target_pairs={{0,1},{1,64},{64,65},{65,0},{2,3},{3,66},{66,67},{67,2},{4,5},{5,6... | collective-permute-start | bytes 393224 | tf_op jit(solution)/shard_map/ppermute | solution.py:387
  19.7 9.0 %collective-permute-start.6 = (bf16[8,128,128]{2,1,0:T(8,128)(2,1)S(1)}, bf16[8,128,128]{2,1,0:T(8,128)(2,1)S(1)}, u32[]{:S(2)}, u32[]{:S(2)}) collective-permute-start(bf16[8,128,128]{2,1,0:T(8,128)(2,1)S(1)} %get-tuple-element.127.refs_0_), channel_id=1, source_target_pairs={{0,6},{2,0},{4,2},{6,4},{1,7},{3,1},{5,3},{7,5},{8,14},{10,8},{12,... | collective-permute-start | bytes 786440 | tf_op jit(solution)/shard_map/ppermute | solution.py:387
  26.0 8.9 %collective-permute-start.8 = (bf16[8,128,128]{2,1,0:T(8,128)(2,1)S(1)}, bf16[8,128,128]{2,1,0:T(8,128)(2,1)S(1)}, u32[]{:S(2)}, u32[]{:S(2)}) collective-permute-start(bf16[8,128,128]{2,1,0:T(8,128)(2,1)S(1)} %get-tuple-element.128.refs_5_), channel_id=1, source_target_pairs={{0,8},{8,16},{16,24},{24,0},{1,9},{9,17},{17,25},{25,1},{2,10},{10... | collective-permute-start | bytes 786440 | tf_op jit(solution)/shard_map/ppermute | solution.py:387
  40.7 21.7 %collective-permute-start.14 = (bf16[32,128,128]{2,1,0:T(8,128)(2,1)S(1)}, bf16[32,128,128]{2,1,0:T(8,128)(2,1)S(1)}, u32[]{:S(2)}, u32[]{:S(2)}) collective-permute-start(bf16[32,128,128]{2,1,0:T(8,128)(2,1)S(1)} %get-tuple-element.129.w0.refs_10_), channel_id=1, source_target_pairs={{0,24},{8,0},{16,8},{24,16},{1,25},{9,1},{17,9},{25,17},{2,26},{10... | collective-permute-start | bytes 3145736 | tf_op jit(solution)/shard_map/ppermute | solution.py:387
  40.8 23.2 %collective-permute-start.12 = (bf16[32,128,128]{2,1,0:T(8,128)(2,1)S(1)}, bf16[32,128,128]{2,1,0:T(8,128)(2,1)S(1)}, u32[]{:S(2)}, u32[]{:S(2)}) collective-permute-start(bf16[32,128,128]{2,1,0:T(8,128)(2,1)S(1)} %get-tuple-element.129.w0.refs_10_), channel_id=1, source_target_pairs={{0,8},{8,16},{16,24},{24,0},{1,9},{9,17},{17,25},{25,1},{2,10},{10... | collective-permute-start | bytes 3145736 | tf_op jit(solution)/shard_map/ppermute | solution.py:387
  42.2 21.9 %collective-permute-start.19 = (bf16[32,128,128]{2,1,0:T(8,128)(2,1)S(1)}, bf16[32,128,128]{2,1,0:T(8,128)(2,1)S(1)}, u32[]{:S(2)}, u32[]{:S(2)}) collective-permute-start(bf16[32,128,128]{2,1,0:T(8,128)(2,1)S(1)} %get-tuple-element.133.l0.refs_15_), channel_id=1, source_target_pairs={{0,6},{2,0},{4,2},{6,4},{1,7},{3,1},{5,3},{7,5},{8,14},{10,8},{12,... | collective-permute-start | bytes 3145736 | tf_op jit(solution)/shard_map/ppermute | solution.py:387
  44.9 22.1 %collective-permute-start.17 = (bf16[32,128,128]{2,1,0:T(8,128)(2,1)S(1)}, bf16[32,128,128]{2,1,0:T(8,128)(2,1)S(1)}, u32[]{:S(2)}, u32[]{:S(2)}) collective-permute-start(bf16[32,128,128]{2,1,0:T(8,128)(2,1)S(1)} %get-tuple-element.133.l0.refs_15_), channel_id=1, source_target_pairs={{0,2},{2,4},{4,6},{6,0},{1,3},{3,5},{5,7},{7,1},{8,10},{10,12},{12... | collective-permute-start | bytes 3145736 | tf_op jit(solution)/shard_map/ppermute | solution.py:387
  62.4 11.0 %collective-permute-start.15 = (bf16[17,128,128]{2,1,0:T(8,128)(2,1)S(1)}, bf16[17,128,128]{2,1,0:T(8,128)(2,1)S(1)}, u32[]{:S(2)}, u32[]{:S(2)}) collective-permute-start(bf16[17,128,128]{2,1,0:T(8,128)(2,1)S(1)} %slice.53), channel_id=1, source_target_pairs={{0,24},{8,0},{16,8},{24,16},{1,25},{9,1},{17,9},{25,17},{2,26},{10... | collective-permute-start | bytes 1671176 | tf_op jit(solution)/shard_map/ppermute | solution.py:387
  64.0 11.4 %collective-permute-start.13 = (bf16[17,128,128]{2,1,0:T(8,128)(2,1)S(1)}, bf16[17,128,128]{2,1,0:T(8,128)(2,1)S(1)}, u32[]{:S(2)}, u32[]{:S(2)}) collective-permute-start(bf16[17,128,128]{2,1,0:T(8,128)(2,1)S(1)} %slice.52), channel_id=1, source_target_pairs={{0,8},{8,16},{16,24},{24,0},{1,9},{9,17},{17,25},{25,1},{2,10},{10... | collective-permute-start | bytes 1671176 | tf_op jit(solution)/shard_map/ppermute | solution.py:387
  64.1 17.4 %collective-permute-start.20 = (bf16[17,128,128]{2,1,0:T(8,128)(2,1)S(1)}, bf16[17,128,128]{2,1,0:T(8,128)(2,1)S(1)}, u32[]{:S(2)}, u32[]{:S(2)}) collective-permute-start(bf16[17,128,128]{2,1,0:T(8,128)(2,1)S(1)} %slice.55), channel_id=1, source_target_pairs={{0,6},{2,0},{4,2},{6,4},{1,7},{3,1},{5,3},{7,5},{8,14},{10,8},{12,... | collective-permute-start | bytes 1671176 | tf_op jit(solution)/shard_map/ppermute | solution.py:387
  67.0 14.5 %collective-permute-start.18 = (bf16[17,128,128]{2,1,0:T(8,128)(2,1)S(1)}, bf16[17,128,128]{2,1,0:T(8,128)(2,1)S(1)}, u32[]{:S(2)}, u32[]{:S(2)}) collective-permute-start(bf16[17,128,128]{2,1,0:T(8,128)(2,1)S(1)} %slice.54), channel_id=1, source_target_pairs={{0,2},{2,4},{4,6},{6,0},{1,3},{3,5},{5,7},{7,1},{8,10},{10,12},{12... | collective-permute-start | bytes 1671176 | tf_op jit(solution)/shard_map/ppermute | solution.py:387
  108.4 11.9 %collective-permute-start.26 = (bf16[2064,128]{1,0:T(8,128)(2,1)S(1)}, bf16[2064,128]{1,0:T(8,128)(2,1)S(1)}, u32[]{:S(2)}, u32[]{:S(2)}) collective-permute-start(bf16[2064,128]{1,0:T(8,128)(2,1)S(1)} %get-tuple-element.201), channel_id=1, source_target_pairs={{0,32},{32,0},{1,33},{33,1},{2,34},{34,2},{3,35},{35,3},{4,36},{36... | collective-permute-start | bytes 1585160 | tf_op jit(solution)/shard_map/ppermute | solution.py:383
  125.3 14.6 %collective-permute-start.33 = (bf16[16,128,128]{2,1,0:T(8,128)(2,1)S(1)}, bf16[16,128,128]{2,1,0:T(8,128)(2,1)S(1)}, u32[]{:S(2)}, u32[]{:S(2)}) collective-permute-start(bf16[16,128,128]{2,1,0:T(8,128)(2,1)S(1)} %get-tuple-element.243), channel_id=1, source_target_pairs={{0,2},{2,4},{4,6},{6,0},{1,3},{3,5},{5,7},{7,1},{8,10},{10,12},{12... | collective-permute-start | bytes 1572872 | tf_op jit(solution)/shard_map/ppermute | solution.py:387
  125.4 14.6 %collective-permute-start.32 = (bf16[16,128,128]{2,1,0:T(8,128)(2,1)S(1)}, bf16[16,128,128]{2,1,0:T(8,128)(2,1)S(1)}, u32[]{:S(2)}, u32[]{:S(2)}) collective-permute-start(bf16[16,128,128]{2,1,0:T(8,128)(2,1)S(1)} %get-tuple-element.244), channel_id=1, source_target_pairs={{0,6},{2,0},{4,2},{6,4},{1,7},{3,1},{5,3},{7,5},{8,14},{10,8},{12,... | collective-permute-start | bytes 1572872 | tf_op jit(solution)/shard_map/ppermute | solution.py:387
  129.6 14.0 %collective-permute-start.29 = (bf16[16,128,128]{2,1,0:T(8,128)(2,1)S(1)}, bf16[16,128,128]{2,1,0:T(8,128)(2,1)S(1)}, u32[]{:S(2)}, u32[]{:S(2)}) collective-permute-start(bf16[16,128,128]{2,1,0:T(8,128)(2,1)S(1)} %get-tuple-element.245), channel_id=1, source_target_pairs={{0,8},{8,16},{16,24},{24,0},{1,9},{9,17},{17,25},{25,1},{2,10},{10... | collective-permute-start | bytes 1572872 | tf_op jit(solution)/shard_map/ppermute | solution.py:387
  129.7 13.9 %collective-permute-start.28 = (bf16[16,128,128]{2,1,0:T(8,128)(2,1)S(1)}, bf16[16,128,128]{2,1,0:T(8,128)(2,1)S(1)}, u32[]{:S(2)}, u32[]{:S(2)}) collective-permute-start(bf16[16,128,128]{2,1,0:T(8,128)(2,1)S(1)} %get-tuple-element.246), channel_id=1, source_target_pairs={{0,24},{8,0},{16,8},{24,16},{1,25},{9,1},{17,9},{25,17},{2,26},{10... | collective-permute-start | bytes 1572872 | tf_op jit(solution)/shard_map/ppermute | solution.py:387
  140.8 23.8 %collective-permute-start.34 = (bf16[32,128,128]{2,1,0:T(8,128)(2,1)S(1)}, bf16[32,128,128]{2,1,0:T(8,128)(2,1)S(1)}, u32[]{:S(2)}, u32[]{:S(2)}) collective-permute-start(bf16[32,128,128]{2,1,0:T(8,128)(2,1)S(1)} %get-tuple-element.224), channel_id=1, source_target_pairs={{0,6},{2,0},{4,2},{6,4},{1,7},{3,1},{5,3},{7,5},{8,14},{10,8},{12,... | collective-permute-start | bytes 3145736 | tf_op jit(solution)/shard_map/ppermute | solution.py:387
  143.2 24.3 %collective-permute-start.35 = (bf16[32,128,128]{2,1,0:T(8,128)(2,1)S(1)}, bf16[32,128,128]{2,1,0:T(8,128)(2,1)S(1)}, u32[]{:S(2)}, u32[]{:S(2)}) collective-permute-start(bf16[32,128,128]{2,1,0:T(8,128)(2,1)S(1)} %get-tuple-element.225), channel_id=1, source_target_pairs={{0,2},{2,4},{4,6},{6,0},{1,3},{3,5},{5,7},{7,1},{8,10},{10,12},{12... | collective-permute-start | bytes 3145736 | tf_op jit(solution)/shard_map/ppermute | solution.py:387
  144.4 23.1 %collective-permute-start.30 = (bf16[32,128,128]{2,1,0:T(8,128)(2,1)S(1)}, bf16[32,128,128]{2,1,0:T(8,128)(2,1)S(1)}, u32[]{:S(2)}, u32[]{:S(2)}) collective-permute-start(bf16[32,128,128]{2,1,0:T(8,128)(2,1)S(1)} %get-tuple-element.218), channel_id=1, source_target_pairs={{0,24},{8,0},{16,8},{24,16},{1,25},{9,1},{17,9},{25,17},{2,26},{10... | collective-permute-start | bytes 3145736 | tf_op jit(solution)/shard_map/ppermute | solution.py:387
  146.8 23.7 %collective-permute-start.31 = (bf16[32,128,128]{2,1,0:T(8,128)(2,1)S(1)}, bf16[32,128,128]{2,1,0:T(8,128)(2,1)S(1)}, u32[]{:S(2)}, u32[]{:S(2)}) collective-permute-start(bf16[32,128,128]{2,1,0:T(8,128)(2,1)S(1)} %get-tuple-element.219), channel_id=1, source_target_pairs={{0,8},{8,16},{16,24},{24,0},{1,9},{9,17},{17,25},{25,1},{2,10},{10... | collective-permute-start | bytes 3145736 | tf_op jit(solution)/shard_map/ppermute | solution.py:387
  174.0 14.1 %collective-permute-start.38 = (bf16[2,4,128,128]{3,2,1,0:T(8,128)(2,1)S(1)}, bf16[2,4,128,128]{3,2,1,0:T(8,128)(2,1)S(1)}, u32[]{:S(2)}, u32[]{:S(2)}) collective-permute-start(bf16[2,4,128,128]{3,2,1,0:T(8,128)(2,1)S(1)} %get-tuple-element.229), channel_id=1, source_target_pairs={{0,2},{2,4},{4,6},{6,0},{1,3},{3,5},{5,7},{7,1},{8,10},{10,12},{12... | collective-permute-start | bytes 786440 | tf_op jit(solution)/shard_map/ppermute | solution.py:387
  174.6 13.5 %collective-permute-start.39 = (bf16[2,4,128,128]{3,2,1,0:T(8,128)(2,1)S(1)}, bf16[2,4,128,128]{3,2,1,0:T(8,128)(2,1)S(1)}, u32[]{:S(2)}, u32[]{:S(2)}) collective-permute-start(bf16[2,4,128,128]{3,2,1,0:T(8,128)(2,1)S(1)} %get-tuple-element.231), channel_id=1, source_target_pairs={{0,24},{8,0},{16,8},{24,16},{1,25},{9,1},{17,9},{25,17},{2,26},{10... | collective-permute-start | bytes 786440 | tf_op jit(solution)/shard_map/ppermute | solution.py:387
  174.9 13.2 %collective-permute-start.40 = (bf16[2,4,128,128]{3,2,1,0:T(8,128)(2,1)S(1)}, bf16[2,4,128,128]{3,2,1,0:T(8,128)(2,1)S(1)}, u32[]{:S(2)}, u32[]{:S(2)}) collective-permute-start(bf16[2,4,128,128]{3,2,1,0:T(8,128)(2,1)S(1)} %get-tuple-element.232), channel_id=1, source_target_pairs={{0,16},{8,24},{16,0},{24,8},{1,17},{9,25},{17,1},{25,9},{2,18},{10... | collective-permute-start | bytes 786440 | tf_op jit(solution)/shard_map/ppermute | solution.py:387
  179.5 9.5 %collective-permute-start.41 = (bf16[2,4,128,128]{3,2,1,0:T(8,128)(2,1)S(1)}, bf16[2,4,128,128]{3,2,1,0:T(8,128)(2,1)S(1)}, u32[]{:S(2)}, u32[]{:S(2)}) collective-permute-start(bf16[2,4,128,128]{3,2,1,0:T(8,128)(2,1)S(1)} %get-tuple-element.233), channel_id=1, source_target_pairs={{0,8},{8,16},{16,24},{24,0},{1,9},{9,17},{17,25},{25,1},{2,10},{10... | collective-permute-start | bytes 786440 | tf_op jit(solution)/shard_map/ppermute | solution.py:387
  (29 other events, 306.9 us)

commit v2 on v1

--- a/solution.py
+++ b/solution.py
@@ -363,7 +363,7 @@
 ACT = kept(ROWS, TOK)
 STATS = kept(8, TOK, dtype=F32)
 SLAB = kept(32, BS, BS)
-SCRATCH = (pltpu.VMEM((2, HALF + 64, TOK), F32),)
+SCRATCH = (pltpu.VMEM((2, HALF + 128, TOK), F32),)
 
 
 def call(kernel, place, ins, outs, scratch=(), old=()):

time: 210 us -> 210 us (level)
  no operation moved by 1% of the time
where the time goes in v2:
time: 210 us; the launch traced here: 207 us
  waiting for transfers between devices  98.9 us (47%)
  starting transfers between devices  65.9 us (31%)
  Pallas kernels  37.9 us (18%)
  local copies, waits for them, and re-layouts  2.8 us (1%)
    ppermute x36, waiting for transfers between devices, ring(): return lax.ppermute(value, axes, [(i, (i + steps) % 4) for i in range(4)])  90.7 us
    ppermute x36, starting transfers between devices, ring(): return lax.ppermute(value, axes, [(i, (i + steps) % 4) for i in range(4)])  40.7 us
    pallas_call x16, Pallas kernels, call(): pl.pallas_call(kernel, out_shape=outs, in_specs=[WHOLE] * len(old) + [SCA...  25.7 us
    ppermute x10, starting transfers between devices, swapped(): return lax.ppermute(value, 'c', SWAP)  25.2 us
    pallas_call x5, Pallas kernels, call_into(): pl.pallas_call(kernel, out_shape=outs, in_specs=[WHOLE] * len(old) + [SCA...  9.22 us
    ppermute x10, waiting for transfers between devices, swapped(): return lax.ppermute(value, 'c', SWAP)  8.21 us
  transfers between devices with their start and end apart: 46, of which 28 were waited for; matrix products, arithmetic and copies ran while one was open for 0% of the time, Pallas kernels for 7%

profile of v2, /device:TPU:1, one launch (start us, length us, event | category | flops | bytes accessed | tf_op | source)
XLA Modules:
  0.0 206.7 jit_solution(12396863145782520480)
XLA Ops:
  6.5 2.9 %collective-permute-start.3 = (bf16[2,2,128,128]{3,2,1,0:T(8,128)(2,1)S(1)}, bf16[2,2,128,128]{3,2,1,0:T(8,128)(2,1)S(1)}, u32[]{:S(2)}, u32[]{:S(2)}) collective-permute-start(bf16[2,2,128,128]{3,2,1,0:T(8,128)(2,1)S(1)} %pad_maximum_fusion.p0), channel_id=1, source_target_pairs={{0,65},{1,0},{64,1},{65,64},{2,67},{3,2},{66,3},{67,66},{4,69},{5,... | collective-permute-start | bytes 393224 | tf_op jit(solution)/shard_map/ppermute | solution.py:387
  10.4 4.2 %collective-permute-done.3.p3 = bf16[2,2,128,128]{3,2,1,0:T(8,128)(2,1)S(1)} collective-permute-done((bf16[2,2,128,128]{3,2,1,0:T(8,128)(2,1)S(1)}, bf16[2,2,128,128]{3,2,1,0:T(8,128)(2,1)S(1)}, u32[]{:S(2)}, u32[]{:S(2)}) %collective-permute-start.3) | collective-permute-done | bytes 131104 | tf_op jit(solution)/shard_map/ppermute | solution.py:387
  15.3 3.8 %collective-permute-done.1.p1 = bf16[2,2,128,128]{3,2,1,0:T(8,128)(2,1)S(1)} collective-permute-done((bf16[2,2,128,128]{3,2,1,0:T(8,128)(2,1)S(1)}, bf16[2,2,128,128]{3,2,1,0:T(8,128)(2,1)S(1)}, u32[]{:S(2)}, u32[]{:S(2)}) %collective-permute-start.1) | collective-permute-done | bytes 131104 | tf_op jit(solution)/shard_map/ppermute | solution.py:387
  19.7 3.8 %collective-permute-start.6 = (bf16[8,128,128]{2,1,0:T(8,128)(2,1)S(1)}, bf16[8,128,128]{2,1,0:T(8,128)(2,1)S(1)}, u32[]{:S(2)}, u32[]{:S(2)}) collective-permute-start(bf16[8,128,128]{2,1,0:T(8,128)(2,1)S(1)} %get-tuple-element.127.refs_0_), channel_id=1, source_target_pairs={{0,6},{2,0},{4,2},{6,4},{1,7},{3,1},{5,3},{7,5},{8,14},{10,8},{12,... | collective-permute-start | bytes 786440 | tf_op jit(solution)/shard_map/ppermute | solution.py:387
  26.0 2.7 %collective-permute-done.6.refs_4_ = bf16[8,128,128]{2,1,0:T(8,128)(2,1)S(1)} collective-permute-done((bf16[8,128,128]{2,1,0:T(8,128)(2,1)S(1)}, bf16[8,128,128]{2,1,0:T(8,128)(2,1)S(1)}, u32[]{:S(2)}, u32[]{:S(2)}) %collective-permute-start.6) | collective-permute-done | bytes 262176 | tf_op jit(solution)/shard_map/ppermute | solution.py:387
  28.7 3.5 %collective-permute-start.7 = (bf16[4,128,128]{2,1,0:T(8,128)(2,1)S(1)}, bf16[4,128,128]{2,1,0:T(8,128)(2,1)S(1)}, u32[]{:S(2)}, u32[]{:S(2)}) collective-permute-start(bf16[4,128,128]{2,1,0:T(8,128)(2,1)S(1)} %slice.49), channel_id=1, source_target_pairs={{0,6},{2,0},{4,2},{6,4},{1,7},{3,1},{5,3},{7,5},{8,14},{10,8},{12,... | collective-permute-start | bytes 393224 | tf_op jit(solution)/shard_map/ppermute | solution.py:387
  37.3 2.7 %collective-permute-done.9.refs_7_ = bf16[4,128,128]{2,1,0:T(8,128)(2,1)S(1)} collective-permute-done((bf16[4,128,128]{2,1,0:T(8,128)(2,1)S(1)}, bf16[4,128,128]{2,1,0:T(8,128)(2,1)S(1)}, u32[]{:S(2)}, u32[]{:S(2)}) %collective-permute-start.9) | collective-permute-done | bytes 131104 | tf_op jit(solution)/shard_map/ppermute | solution.py:387
  44.9 17.5 %collective-permute-done.14.w4.refs_14_ = bf16[32,128,128]{2,1,0:T(8,128)(2,1)S(1)} collective-permute-done((bf16[32,128,128]{2,1,0:T(8,128)(2,1)S(1)}, bf16[32,128,128]{2,1,0:T(8,128)(2,1)S(1)}, u32[]{:S(2)}, u32[]{:S(2)}) %collective-permute-start.14) | collective-permute-done | bytes 1048608 | tf_op jit(solution)/shard_map/ppermute | solution.py:387
  64.1 2.8 %collective-permute-start.20 = (bf16[17,128,128]{2,1,0:T(8,128)(2,1)S(1)}, bf16[17,128,128]{2,1,0:T(8,128)(2,1)S(1)}, u32[]{:S(2)}, u32[]{:S(2)}) collective-permute-start(bf16[17,128,128]{2,1,0:T(8,128)(2,1)S(1)} %slice.55), channel_id=1, source_target_pairs={{0,6},{2,0},{4,2},{6,4},{1,7},{3,1},{5,3},{7,5},{8,14},{10,8},{12,... | collective-permute-start | bytes 1671176 | tf_op jit(solution)/shard_map/ppermute | solution.py:387
  69.1 4.3 %collective-permute-done.15.w3.refs_13_ = bf16[17,128,128]{2,1,0:T(8,128)(2,1)S(1)} collective-permute-done((bf16[17,128,128]{2,1,0:T(8,128)(2,1)S(1)}, bf16[17,128,128]{2,1,0:T(8,128)(2,1)S(1)}, u32[]{:S(2)}, u32[]{:S(2)}) %collective-permute-start.15) | collective-permute-done | bytes 557088 | tf_op jit(solution)/shard_map/ppermute | solution.py:387
  76.6 5.0 %collective-permute-start.16 = (bf16[2064,128]{1,0:T(8,128)(2,1)S(1)}, bf16[2064,128]{1,0:T(8,128)(2,1)S(1)}, u32[]{:S(2)}, u32[]{:S(2)}) collective-permute-start(bf16[2064,128]{1,0:T(8,128)(2,1)S(1)} %get-tuple-element.131), channel_id=1, source_target_pairs={{0,32},{32,0},{1,33},{33,1},{2,34},{34,2},{3,35},{35,3},{4,36},{36... | collective-permute-start | bytes 1585160 | tf_op jit(solution)/shard_map/ppermute | solution.py:383
  83.1 2.7 %shard_map.81 = (bf16[4096,128]{1,0:T(8,128)(2,1)S(1)}, bf16[4096,128]{1,0:T(8,128)(2,1)S(1)}, bf16[4096,128]{1,0:T(8,128)(2,1)S(1)}, f32[8,128]{1,0:T(8,128)S(1...) custom-call(s32[5]{0:T(128)S(1)} %stack.32.place_ref.refs_0_.refs_4_.refs_8_, ...), custom_call_target="tpu_custom_call" | custom-call | tf_op jit(solution)/shard_map/pallas_call | solution.py:372
  88.1 2.7 %shard_map.82 = (bf16[4096,128]{1,0:T(8,128)(2,1)S(1)}, bf16[4096,128]{1,0:T(8,128)(2,1)S(1)}, bf16[4096,128]{1,0:T(8,128)(2,1)S(1)}, f32[8,128]{1,0:T(8,128)S(1...) custom-call(s32[5]{0:T(128)S(1)} %stack.32.place_ref.refs_0_.refs_4_.refs_8_, ...), custom_call_target="tpu_custom_call" | custom-call | tf_op jit(solution)/shard_map/pallas_call | solution.py:372
  92.8 2.7 %shard_map.83 = (bf16[4096,128]{1,0:T(8,128)(2,1)S(1)}, bf16[4096,128]{1,0:T(8,128)(2,1)S(1)}, bf16[4096,128]{1,0:T(8,128)(2,1)S(1)}, f32[8,128]{1,0:T(8,128)S(1...) custom-call(s32[5]{0:T(128)S(1)} %stack.32.place_ref.refs_0_.refs_4_.refs_8_, ...), custom_call_target="tpu_custom_call" | custom-call | tf_op jit(solution)/shard_map/pallas_call | solution.py:372
  108.4 9.7 %collective-permute-start.26 = (bf16[2064,128]{1,0:T(8,128)(2,1)S(1)}, bf16[2064,128]{1,0:T(8,128)(2,1)S(1)}, u32[]{:S(2)}, u32[]{:S(2)}) collective-permute-start(bf16[2064,128]{1,0:T(8,128)(2,1)S(1)} %get-tuple-element.201), channel_id=1, source_target_pairs={{0,32},{32,0},{1,33},{33,1},{2,34},{34,2},{3,35},{35,3},{4,36},{36... | collective-permute-start | bytes 1585160 | tf_op jit(solution)/shard_map/ppermute | solution.py:383
  125.4 2.7 %collective-permute-start.32 = (bf16[16,128,128]{2,1,0:T(8,128)(2,1)S(1)}, bf16[16,128,128]{2,1,0:T(8,128)(2,1)S(1)}, u32[]{:S(2)}, u32[]{:S(2)}) collective-permute-start(bf16[16,128,128]{2,1,0:T(8,128)(2,1)S(1)} %get-tuple-element.244), channel_id=1, source_target_pairs={{0,6},{2,0},{4,2},{6,4},{1,7},{3,1},{5,3},{7,5},{8,14},{10,8},{12,... | collective-permute-start | bytes 1572872 | tf_op jit(solution)/shard_map/ppermute | solution.py:387
  129.7 2.7 %collective-permute-start.28 = (bf16[16,128,128]{2,1,0:T(8,128)(2,1)S(1)}, bf16[16,128,128]{2,1,0:T(8,128)(2,1)S(1)}, u32[]{:S(2)}, u32[]{:S(2)}) collective-permute-start(bf16[16,128,128]{2,1,0:T(8,128)(2,1)S(1)} %get-tuple-element.246), channel_id=1, source_target_pairs={{0,24},{8,0},{16,8},{24,16},{1,25},{9,1},{17,9},{25,17},{2,26},{10... | collective-permute-start | bytes 1572872 | tf_op jit(solution)/shard_map/ppermute | solution.py:387
  132.3 7.7 %collective-permute-done.33.hi_ref = bf16[16,128,128]{2,1,0:T(8,128)(2,1)S(1)} collective-permute-done((bf16[16,128,128]{2,1,0:T(8,128)(2,1)S(1)}, bf16[16,128,128]{2,1,0:T(8,128)(2,1)S(1)}, u32[]{:S(2)}, u32[]{:S(2)}) %collective-permute-start.33) | collective-permute-done | bytes 524320 | tf_op jit(solution)/shard_map/ppermute | solution.py:387
  146.8 17.7 %collective-permute-done.34.refs_4_ = bf16[32,128,128]{2,1,0:T(8,128)(2,1)S(1)} collective-permute-done((bf16[32,128,128]{2,1,0:T(8,128)(2,1)S(1)}, bf16[32,128,128]{2,1,0:T(8,128)(2,1)S(1)}, u32[]{:S(2)}, u32[]{:S(2)}) %collective-permute-start.34) | collective-permute-done | bytes 1048608 | tf_op jit(solution)/shard_map/ppermute | solution.py:387
  164.6 3.0 %collective-permute-done.35.refs_5_ = bf16[32,128,128]{2,1,0:T(8,128)(2,1)S(1)} collective-permute-done((bf16[32,128,128]{2,1,0:T(8,128)(2,1)S(1)}, bf16[32,128,128]{2,1,0:T(8,128)(2,1)S(1)}, u32[]{:S(2)}, u32[]{:S(2)}) %collective-permute-start.35) | collective-permute-done | bytes 1048608 | tf_op jit(solution)/shard_map/ppermute | solution.py:387
  167.5 3.0 %collective-permute-done.31.refs_2_ = bf16[32,128,128]{2,1,0:T(8,128)(2,1)S(1)} collective-permute-done((bf16[32,128,128]{2,1,0:T(8,128)(2,1)S(1)}, bf16[32,128,128]{2,1,0:T(8,128)(2,1)S(1)}, u32[]{:S(2)}, u32[]{:S(2)}) %collective-permute-start.31) | collective-permute-done | bytes 1048608 | tf_op jit(solution)/shard_map/ppermute | solution.py:387
  175.5 4.0 %collective-permute-done.36.refs_1_ = bf16[2,4,128,128]{3,2,1,0:T(8,128)(2,1)S(1)} collective-permute-done((bf16[2,4,128,128]{3,2,1,0:T(8,128)(2,1)S(1)}, bf16[2,4,128,128]{3,2,1,0:T(8,128)(2,1)S(1)}, u32[]{:S(2)}, u32[]{:S(2)}) %collective-permute-start.36) | collective-permute-done | bytes 262176 | tf_op jit(solution)/shard_map/ppermute | solution.py:387
  180.8 7.3 %collective-permute-done.38.refs_3_ = bf16[2,4,128,128]{3,2,1,0:T(8,128)(2,1)S(1)} collective-permute-done((bf16[2,4,128,128]{3,2,1,0:T(8,128)(2,1)S(1)}, bf16[2,4,128,128]{3,2,1,0:T(8,128)(2,1)S(1)}, u32[]{:S(2)}, u32[]{:S(2)}) %collective-permute-start.38) | collective-permute-done | bytes 262176 | tf_op jit(solution)/shard_map/ppermute | solution.py:387
  197.3 6.0 %collective-permute-start.45 = (f32[2,128,128]{2,1,0:T(8,128)S(1)}, f32[2,128,128]{2,1,0:T(8,128)S(1)}, u32[]{:S(2)}, u32[]{:S(2)}) collective-permute-start(f32[2,128,128]{2,1,0:T(8,128)S(1)} %get-tuple-element.239), channel_id=1, source_target_pairs={{0,32},{32,0},{1,33},{33,1},{2,34},{34,2},{3,35},{35,3},{4,36},{36... | collective-permute-start | bytes 393224 | tf_op jit(solution)/shard_map/ppermute | solution.py:383
  (117 shorter events, 80.8 us)
Async XLA Ops:
  9.7 9.4 %collective-permute-start.1 = (bf16[2,2,128,128]{3,2,1,0:T(8,128)(2,1)S(1)}, bf16[2,2,128,128]{3,2,1,0:T(8,128)(2,1)S(1)}, u32[]{:S(2)}, u32[]{:S(2)}) collective-permute-start(bf16[2,2,128,128]{3,2,1,0:T(8,128)(2,1)S(1)} %pad_maximum_fusion.p0), channel_id=1, source_target_pairs={{0,1},{1,64},{64,65},{65,0},{2,3},{3,66},{66,67},{67,2},{4,5},{5,6... | collective-permute-start | bytes 393224 | tf_op jit(solution)/shard_map/ppermute | solution.py:387
  19.7 9.0 %collective-permute-start.6 = (bf16[8,128,128]{2,1,0:T(8,128)(2,1)S(1)}, bf16[8,128,128]{2,1,0:T(8,128)(2,1)S(1)}, u32[]{:S(2)}, u32[]{:S(2)}) collective-permute-start(bf16[8,128,128]{2,1,0:T(8,128)(2,1)S(1)} %get-tuple-element.127.refs_0_), channel_id=1, source_target_pairs={{0,6},{2,0},{4,2},{6,4},{1,7},{3,1},{5,3},{7,5},{8,14},{10,8},{12,... | collective-permute-start | bytes 786440 | tf_op jit(solution)/shard_map/ppermute | solution.py:387
  26.0 8.9 %collective-permute-start.8 = (bf16[8,128,128]{2,1,0:T(8,128)(2,1)S(1)}, bf16[8,128,128]{2,1,0:T(8,128)(2,1)S(1)}, u32[]{:S(2)}, u32[]{:S(2)}) collective-permute-start(bf16[8,128,128]{2,1,0:T(8,128)(2,1)S(1)} %get-tuple-element.128.refs_5_), channel_id=1, source_target_pairs={{0,8},{8,16},{16,24},{24,0},{1,9},{9,17},{17,25},{25,1},{2,10},{10... | collective-permute-start | bytes 786440 | tf_op jit(solution)/shard_map/ppermute | solution.py:387
  40.7 21.7 %collective-permute-start.14 = (bf16[32,128,128]{2,1,0:T(8,128)(2,1)S(1)}, bf16[32,128,128]{2,1,0:T(8,128)(2,1)S(1)}, u32[]{:S(2)}, u32[]{:S(2)}) collective-permute-start(bf16[32,128,128]{2,1,0:T(8,128)(2,1)S(1)} %get-tuple-element.129.w0.refs_10_), channel_id=1, source_target_pairs={{0,24},{8,0},{16,8},{24,16},{1,25},{9,1},{17,9},{25,17},{2,26},{10... | collective-permute-start | bytes 3145736 | tf_op jit(solution)/shard_map/ppermute | solution.py:387
  40.8 23.2 %collective-permute-start.12 = (bf16[32,128,128]{2,1,0:T(8,128)(2,1)S(1)}, bf16[32,128,128]{2,1,0:T(8,128)(2,1)S(1)}, u32[]{:S(2)}, u32[]{:S(2)}) collective-permute-start(bf16[32,128,128]{2,1,0:T(8,128)(2,1)S(1)} %get-tuple-element.129.w0.refs_10_), channel_id=1, source_target_pairs={{0,8},{8,16},{16,24},{24,0},{1,9},{9,17},{17,25},{25,1},{2,10},{10... | collective-permute-start | bytes 3145736 | tf_op jit(solution)/shard_map/ppermute | solution.py:387
  42.2 21.9 %collective-permute-start.19 = (bf16[32,128,128]{2,1,0:T(8,128)(2,1)S(1)}, bf16[32,128,128]{2,1,0:T(8,128)(2,1)S(1)}, u32[]{:S(2)}, u32[]{:S(2)}) collective-permute-start(bf16[32,128,128]{2,1,0:T(8,128)(2,1)S(1)} %get-tuple-element.133.l0.refs_15_), channel_id=1, source_target_pairs={{0,6},{2,0},{4,2},{6,4},{1,7},{3,1},{5,3},{7,5},{8,14},{10,8},{12,... | collective-permute-start | bytes 3145736 | tf_op jit(solution)/shard_map/ppermute | solution.py:387
  44.9 22.1 %collective-permute-start.17 = (bf16[32,128,128]{2,1,0:T(8,128)(2,1)S(1)}, bf16[32,128,128]{2,1,0:T(8,128)(2,1)S(1)}, u32[]{:S(2)}, u32[]{:S(2)}) collective-permute-start(bf16[32,128,128]{2,1,0:T(8,128)(2,1)S(1)} %get-tuple-element.133.l0.refs_15_), channel_id=1, source_target_pairs={{0,2},{2,4},{4,6},{6,0},{1,3},{3,5},{5,7},{7,1},{8,10},{10,12},{12... | collective-permute-start | bytes 3145736 | tf_op jit(solution)/shard_map/ppermute | solution.py:387
  62.4 11.0 %collective-permute-start.15 = (bf16[17,128,128]{2,1,0:T(8,128)(2,1)S(1)}, bf16[17,128,128]{2,1,0:T(8,128)(2,1)S(1)}, u32[]{:S(2)}, u32[]{:S(2)}) collective-permute-start(bf16[17,128,128]{2,1,0:T(8,128)(2,1)S(1)} %slice.53), channel_id=1, source_target_pairs={{0,24},{8,0},{16,8},{24,16},{1,25},{9,1},{17,9},{25,17},{2,26},{10... | collective-permute-start | bytes 1671176 | tf_op jit(solution)/shard_map/ppermute | solution.py:387
  64.0 11.4 %collective-permute-start.13 = (bf16[17,128,128]{2,1,0:T(8,128)(2,1)S(1)}, bf16[17,128,128]{2,1,0:T(8,128)(2,1)S(1)}, u32[]{:S(2)}, u32[]{:S(2)}) collective-permute-start(bf16[17,128,128]{2,1,0:T(8,128)(2,1)S(1)} %slice.52), channel_id=1, source_target_pairs={{0,8},{8,16},{16,24},{24,0},{1,9},{9,17},{17,25},{25,1},{2,10},{10... | collective-permute-start | bytes 1671176 | tf_op jit(solution)/shard_map/ppermute | solution.py:387
  64.1 17.4 %collective-permute-start.20 = (bf16[17,128,128]{2,1,0:T(8,128)(2,1)S(1)}, bf16[17,128,128]{2,1,0:T(8,128)(2,1)S(1)}, u32[]{:S(2)}, u32[]{:S(2)}) collective-permute-start(bf16[17,128,128]{2,1,0:T(8,128)(2,1)S(1)} %slice.55), channel_id=1, source_target_pairs={{0,6},{2,0},{4,2},{6,4},{1,7},{3,1},{5,3},{7,5},{8,14},{10,8},{12,... | collective-permute-start | bytes 1671176 | tf_op jit(solution)/shard_map/ppermute | solution.py:387
  67.0 14.5 %collective-permute-start.18 = (bf16[17,128,128]{2,1,0:T(8,128)(2,1)S(1)}, bf16[17,128,128]{2,1,0:T(8,128)(2,1)S(1)}, u32[]{:S(2)}, u32[]{:S(2)}) collective-permute-start(bf16[17,128,128]{2,1,0:T(8,128)(2,1)S(1)} %slice.54), channel_id=1, source_target_pairs={{0,2},{2,4},{4,6},{6,0},{1,3},{3,5},{5,7},{7,1},{8,10},{10,12},{12... | collective-permute-start | bytes 1671176 | tf_op jit(solution)/shard_map/ppermute | solution.py:387
  108.4 11.9 %collective-permute-start.26 = (bf16[2064,128]{1,0:T(8,128)(2,1)S(1)}, bf16[2064,128]{1,0:T(8,128)(2,1)S(1)}, u32[]{:S(2)}, u32[]{:S(2)}) collective-permute-start(bf16[2064,128]{1,0:T(8,128)(2,1)S(1)} %get-tuple-element.201), channel_id=1, source_target_pairs={{0,32},{32,0},{1,33},{33,1},{2,34},{34,2},{3,35},{35,3},{4,36},{36... | collective-permute-start | bytes 1585160 | tf_op jit(solution)/shard_map/ppermute | solution.py:383
  125.3 14.6 %collective-permute-start.33 = (bf16[16,128,128]{2,1,0:T(8,128)(2,1)S(1)}, bf16[16,128,128]{2,1,0:T(8,128)(2,1)S(1)}, u32[]{:S(2)}, u32[]{:S(2)}) collective-permute-start(bf16[16,128,128]{2,1,0:T(8,128)(2,1)S(1)} %get-tuple-element.243), channel_id=1, source_target_pairs={{0,2},{2,4},{4,6},{6,0},{1,3},{3,5},{5,7},{7,1},{8,10},{10,12},{12... | collective-permute-start | bytes 1572872 | tf_op jit(solution)/shard_map/ppermute | solution.py:387
  125.4 14.6 %collective-permute-start.32 = (bf16[16,128,128]{2,1,0:T(8,128)(2,1)S(1)}, bf16[16,128,128]{2,1,0:T(8,128)(2,1)S(1)}, u32[]{:S(2)}, u32[]{:S(2)}) collective-permute-start(bf16[16,128,128]{2,1,0:T(8,128)(2,1)S(1)} %get-tuple-element.244), channel_id=1, source_target_pairs={{0,6},{2,0},{4,2},{6,4},{1,7},{3,1},{5,3},{7,5},{8,14},{10,8},{12,... | collective-permute-start | bytes 1572872 | tf_op jit(solution)/shard_map/ppermute | solution.py:387
  129.6 14.0 %collective-permute-start.29 = (bf16[16,128,128]{2,1,0:T(8,128)(2,1)S(1)}, bf16[16,128,128]{2,1,0:T(8,128)(2,1)S(1)}, u32[]{:S(2)}, u32[]{:S(2)}) collective-permute-start(bf16[16,128,128]{2,1,0:T(8,128)(2,1)S(1)} %get-tuple-element.245), channel_id=1, source_target_pairs={{0,8},{8,16},{16,24},{24,0},{1,9},{9,17},{17,25},{25,1},{2,10},{10... | collective-permute-start | bytes 1572872 | tf_op jit(solution)/shard_map/ppermute | solution.py:387
  129.7 13.9 %collective-permute-start.28 = (bf16[16,128,128]{2,1,0:T(8,128)(2,1)S(1)}, bf16[16,128,128]{2,1,0:T(8,128)(2,1)S(1)}, u32[]{:S(2)}, u32[]{:S(2)}) collective-permute-start(bf16[16,128,128]{2,1,0:T(8,128)(2,1)S(1)} %get-tuple-element.246), channel_id=1, source_target_pairs={{0,24},{8,0},{16,8},{24,16},{1,25},{9,1},{17,9},{25,17},{2,26},{10... | collective-permute-start | bytes 1572872 | tf_op jit(solution)/shard_map/ppermute | solution.py:387
  140.8 23.8 %collective-permute-start.34 = (bf16[32,128,128]{2,1,0:T(8,128)(2,1)S(1)}, bf16[32,128,128]{2,1,0:T(8,128)(2,1)S(1)}, u32[]{:S(2)}, u32[]{:S(2)}) collective-permute-start(bf16[32,128,128]{2,1,0:T(8,128)(2,1)S(1)} %get-tuple-element.224), channel_id=1, source_target_pairs={{0,6},{2,0},{4,2},{6,4},{1,7},{3,1},{5,3},{7,5},{8,14},{10,8},{12,... | collective-permute-start | bytes 3145736 | tf_op jit(solution)/shard_map/ppermute | solution.py:387
  143.2 24.3 %collective-permute-start.35 = (bf16[32,128,128]{2,1,0:T(8,128)(2,1)S(1)}, bf16[32,128,128]{2,1,0:T(8,128)(2,1)S(1)}, u32[]{:S(2)}, u32[]{:S(2)}) collective-permute-start(bf16[32,128,128]{2,1,0:T(8,128)(2,1)S(1)} %get-tuple-element.225), channel_id=1, source_target_pairs={{0,2},{2,4},{4,6},{6,0},{1,3},{3,5},{5,7},{7,1},{8,10},{10,12},{12... | collective-permute-start | bytes 3145736 | tf_op jit(solution)/shard_map/ppermute | solution.py:387
  144.4 23.1 %collective-permute-start.30 = (bf16[32,128,128]{2,1,0:T(8,128)(2,1)S(1)}, bf16[32,128,128]{2,1,0:T(8,128)(2,1)S(1)}, u32[]{:S(2)}, u32[]{:S(2)}) collective-permute-start(bf16[32,128,128]{2,1,0:T(8,128)(2,1)S(1)} %get-tuple-element.218), channel_id=1, source_target_pairs={{0,24},{8,0},{16,8},{24,16},{1,25},{9,1},{17,9},{25,17},{2,26},{10... | collective-permute-start | bytes 3145736 | tf_op jit(solution)/shard_map/ppermute | solution.py:387
  146.8 23.7 %collective-permute-start.31 = (bf16[32,128,128]{2,1,0:T(8,128)(2,1)S(1)}, bf16[32,128,128]{2,1,0:T(8,128)(2,1)S(1)}, u32[]{:S(2)}, u32[]{:S(2)}) collective-permute-start(bf16[32,128,128]{2,1,0:T(8,128)(2,1)S(1)} %get-tuple-element.219), channel_id=1, source_target_pairs={{0,8},{8,16},{16,24},{24,0},{1,9},{9,17},{17,25},{25,1},{2,10},{10... | collective-permute-start | bytes 3145736 | tf_op jit(solution)/shard_map/ppermute | solution.py:387
  174.0 14.1 %collective-permute-start.38 = (bf16[2,4,128,128]{3,2,1,0:T(8,128)(2,1)S(1)}, bf16[2,4,128,128]{3,2,1,0:T(8,128)(2,1)S(1)}, u32[]{:S(2)}, u32[]{:S(2)}) collective-permute-start(bf16[2,4,128,128]{3,2,1,0:T(8,128)(2,1)S(1)} %get-tuple-element.229), channel_id=1, source_target_pairs={{0,2},{2,4},{4,6},{6,0},{1,3},{3,5},{5,7},{7,1},{8,10},{10,12},{12... | collective-permute-start | bytes 786440 | tf_op jit(solution)/shard_map/ppermute | solution.py:387
  174.6 13.5 %collective-permute-start.39 = (bf16[2,4,128,128]{3,2,1,0:T(8,128)(2,1)S(1)}, bf16[2,4,128,128]{3,2,1,0:T(8,128)(2,1)S(1)}, u32[]{:S(2)}, u32[]{:S(2)}) collective-permute-start(bf16[2,4,128,128]{3,2,1,0:T(8,128)(2,1)S(1)} %get-tuple-element.231), channel_id=1, source_target_pairs={{0,24},{8,0},{16,8},{24,16},{1,25},{9,1},{17,9},{25,17},{2,26},{10... | collective-permute-start | bytes 786440 | tf_op jit(solution)/shard_map/ppermute | solution.py:387
  174.9 13.2 %collective-permute-start.40 = (bf16[2,4,128,128]{3,2,1,0:T(8,128)(2,1)S(1)}, bf16[2,4,128,128]{3,2,1,0:T(8,128)(2,1)S(1)}, u32[]{:S(2)}, u32[]{:S(2)}) collective-permute-start(bf16[2,4,128,128]{3,2,1,0:T(8,128)(2,1)S(1)} %get-tuple-element.232), channel_id=1, source_target_pairs={{0,16},{8,24},{16,0},{24,8},{1,17},{9,25},{17,1},{25,9},{2,18},{10... | collective-permute-start | bytes 786440 | tf_op jit(solution)/shard_map/ppermute | solution.py:387
  179.5 9.5 %collective-permute-start.41 = (bf16[2,4,128,128]{3,2,1,0:T(8,128)(2,1)S(1)}, bf16[2,4,128,128]{3,2,1,0:T(8,128)(2,1)S(1)}, u32[]{:S(2)}, u32[]{:S(2)}) collective-permute-start(bf16[2,4,128,128]{3,2,1,0:T(8,128)(2,1)S(1)} %get-tuple-element.233), channel_id=1, source_target_pairs={{0,8},{8,16},{16,24},{24,0},{1,9},{9,17},{17,25},{25,1},{2,10},{10... | collective-permute-start | bytes 786440 | tf_op jit(solution)/shard_map/ppermute | solution.py:387
  (29 other events, 306.9 us)

commit v3 on v2

--- a/solution.py
+++ b/solution.py
@@ -490,6 +490,7 @@
         )
         factors(layer, below, (go, gr, xs[layer], perms[below], pre))
     factors(0, None, (uo, swapped(us), xs[0]))
+    slabs["right"], slabs["left"] = lax.optimization_barrier((slabs["right"], slabs["left"]))
     outs = call(sum_pair_kernel, place, ring_reduced(slabs["right"], slabs["left"], place), (stage,) * 8)
     parts = scattered(outs[:4], "z") + scattered(outs[4:], "x")
     outs = call(sum_ring_kernel, place, parts, (kept(2, 2, BS, BS),) * 4)

time: 210 us -> 212 us (level)
  transfers between devices with their start and end apart: 46 -> 46, of which waited for: 28 -> 27; matrix products, arithmetic and copies ran while one was open for 0% -> 0% of each run, Pallas kernels for 7% -> 6%
where the time goes in v3:
time: 212 us; the launch traced here: 208 us
  waiting for transfers between devices  100 us (47%)
  starting transfers between devices  66 us (31%)
  Pallas kernels  37.9 us (18%)
  local copies, waits for them, and re-layouts  2.82 us (1%)
    ppermute x36, waiting for transfers between devices, ring(): return lax.ppermute(value, axes, [(i, (i + steps) % 4) for i in range(4)])  92 us
    ppermute x36, starting transfers between devices, ring(): return lax.ppermute(value, axes, [(i, (i + steps) % 4) for i in range(4)])  40.7 us
    pallas_call x16, Pallas kernels, call(): pl.pallas_call(kernel, out_shape=outs, in_specs=[WHOLE] * len(old) + [SCA...  25.7 us
    ppermute x10, starting transfers between devices, swapped(): return lax.ppermute(value, 'c', SWAP)  25.3 us
    pallas_call x5, Pallas kernels, call_into(): pl.pallas_call(kernel, out_shape=outs, in_specs=[WHOLE] * len(old) + [SCA...  9.22 us
    ppermute x10, waiting for transfers between devices, swapped(): return lax.ppermute(value, 'c', SWAP)  8.21 us
  transfers between devices with their start and end apart: 46, of which 27 were waited for; matrix products, arithmetic and copies ran while one was open for 0% of the time, Pallas kernels for 6%

profile of v3, /device:TPU:1, one launch (start us, length us, event | category | flops | bytes accessed | tf_op | source)
XLA Modules:
  0.0 208.1 jit_solution(8379725448494333180)
XLA Ops:
  6.5 2.9 %collective-permute-start.3 = (bf16[2,2,128,128]{3,2,1,0:T(8,128)(2,1)S(1)}, bf16[2,2,128,128]{3,2,1,0:T(8,128)(2,1)S(1)}, u32[]{:S(2)}, u32[]{:S(2)}) collective-permute-start(bf16[2,2,128,128]{3,2,1,0:T(8,128)(2,1)S(1)} %pad_maximum_fusion.p0), channel_id=1, source_target_pairs={{0,65},{1,0},{64,1},{65,64},{2,67},{3,2},{66,3},{67,66},{4,69},{5,... | collective-permute-start | bytes 393224 | tf_op jit(solution)/shard_map/ppermute | solution.py:387
  10.4 4.2 %collective-permute-done.3.p3 = bf16[2,2,128,128]{3,2,1,0:T(8,128)(2,1)S(1)} collective-permute-done((bf16[2,2,128,128]{3,2,1,0:T(8,128)(2,1)S(1)}, bf16[2,2,128,128]{3,2,1,0:T(8,128)(2,1)S(1)}, u32[]{:S(2)}, u32[]{:S(2)}) %collective-permute-start.3) | collective-permute-done | bytes 131104 | tf_op jit(solution)/shard_map/ppermute | solution.py:387
  15.3 3.8 %collective-permute-done.1.p1 = bf16[2,2,128,128]{3,2,1,0:T(8,128)(2,1)S(1)} collective-permute-done((bf16[2,2,128,128]{3,2,1,0:T(8,128)(2,1)S(1)}, bf16[2,2,128,128]{3,2,1,0:T(8,128)(2,1)S(1)}, u32[]{:S(2)}, u32[]{:S(2)}) %collective-permute-start.1) | collective-permute-done | bytes 131104 | tf_op jit(solution)/shard_map/ppermute | solution.py:387
  19.7 3.8 %collective-permute-start.6 = (bf16[8,128,128]{2,1,0:T(8,128)(2,1)S(1)}, bf16[8,128,128]{2,1,0:T(8,128)(2,1)S(1)}, u32[]{:S(2)}, u32[]{:S(2)}) collective-permute-start(bf16[8,128,128]{2,1,0:T(8,128)(2,1)S(1)} %get-tuple-element.135.refs_0_), channel_id=1, source_target_pairs={{0,6},{2,0},{4,2},{6,4},{1,7},{3,1},{5,3},{7,5},{8,14},{10,8},{12,... | collective-permute-start | bytes 786440 | tf_op jit(solution)/shard_map/ppermute | solution.py:387
  26.0 2.7 %collective-permute-done.6.refs_4_ = bf16[8,128,128]{2,1,0:T(8,128)(2,1)S(1)} collective-permute-done((bf16[8,128,128]{2,1,0:T(8,128)(2,1)S(1)}, bf16[8,128,128]{2,1,0:T(8,128)(2,1)S(1)}, u32[]{:S(2)}, u32[]{:S(2)}) %collective-permute-start.6) | collective-permute-done | bytes 262176 | tf_op jit(solution)/shard_map/ppermute | solution.py:387
  28.7 3.5 %collective-permute-start.7 = (bf16[4,128,128]{2,1,0:T(8,128)(2,1)S(1)}, bf16[4,128,128]{2,1,0:T(8,128)(2,1)S(1)}, u32[]{:S(2)}, u32[]{:S(2)}) collective-permute-start(bf16[4,128,128]{2,1,0:T(8,128)(2,1)S(1)} %slice.49), channel_id=1, source_target_pairs={{0,6},{2,0},{4,2},{6,4},{1,7},{3,1},{5,3},{7,5},{8,14},{10,8},{12,... | collective-permute-start | bytes 393224 | tf_op jit(solution)/shard_map/ppermute | solution.py:387
  37.3 2.7 %collective-permute-done.9.refs_7_ = bf16[4,128,128]{2,1,0:T(8,128)(2,1)S(1)} collective-permute-done((bf16[4,128,128]{2,1,0:T(8,128)(2,1)S(1)}, bf16[4,128,128]{2,1,0:T(8,128)(2,1)S(1)}, u32[]{:S(2)}, u32[]{:S(2)}) %collective-permute-start.9) | collective-permute-done | bytes 131104 | tf_op jit(solution)/shard_map/ppermute | solution.py:387
  44.9 17.5 %collective-permute-done.14.w4.refs_14_ = bf16[32,128,128]{2,1,0:T(8,128)(2,1)S(1)} collective-permute-done((bf16[32,128,128]{2,1,0:T(8,128)(2,1)S(1)}, bf16[32,128,128]{2,1,0:T(8,128)(2,1)S(1)}, u32[]{:S(2)}, u32[]{:S(2)}) %collective-permute-start.14) | collective-permute-done | bytes 1048608 | tf_op jit(solution)/shard_map/ppermute | solution.py:387
  64.1 2.8 %collective-permute-start.20 = (bf16[17,128,128]{2,1,0:T(8,128)(2,1)S(1)}, bf16[17,128,128]{2,1,0:T(8,128)(2,1)S(1)}, u32[]{:S(2)}, u32[]{:S(2)}) collective-permute-start(bf16[17,128,128]{2,1,0:T(8,128)(2,1)S(1)} %slice.55), channel_id=1, source_target_pairs={{0,6},{2,0},{4,2},{6,4},{1,7},{3,1},{5,3},{7,5},{8,14},{10,8},{12,... | collective-permute-start | bytes 1671176 | tf_op jit(solution)/shard_map/ppermute | solution.py:387
  69.1 4.3 %collective-permute-done.15.w3.refs_13_ = bf16[17,128,128]{2,1,0:T(8,128)(2,1)S(1)} collective-permute-done((bf16[17,128,128]{2,1,0:T(8,128)(2,1)S(1)}, bf16[17,128,128]{2,1,0:T(8,128)(2,1)S(1)}, u32[]{:S(2)}, u32[]{:S(2)}) %collective-permute-start.15) | collective-permute-done | bytes 557088 | tf_op jit(solution)/shard_map/ppermute | solution.py:387
  76.6 5.0 %collective-permute-start.16 = (bf16[2064,128]{1,0:T(8,128)(2,1)S(1)}, bf16[2064,128]{1,0:T(8,128)(2,1)S(1)}, u32[]{:S(2)}, u32[]{:S(2)}) collective-permute-start(bf16[2064,128]{1,0:T(8,128)(2,1)S(1)} %get-tuple-element.139), channel_id=1, source_target_pairs={{0,32},{32,0},{1,33},{33,1},{2,34},{34,2},{3,35},{35,3},{4,36},{36... | collective-permute-start | bytes 1585160 | tf_op jit(solution)/shard_map/ppermute | solution.py:383
  83.1 2.7 %shard_map.81 = (bf16[4096,128]{1,0:T(8,128)(2,1)S(1)}, bf16[4096,128]{1,0:T(8,128)(2,1)S(1)}, bf16[4096,128]{1,0:T(8,128)(2,1)S(1)}, f32[8,128]{1,0:T(8,128)S(1...) custom-call(s32[5]{0:T(128)S(1)} %stack.32.place_ref.refs_0_.refs_4_.refs_8_, ...), custom_call_target="tpu_custom_call" | custom-call | tf_op jit(solution)/shard_map/pallas_call | solution.py:372
  88.1 2.7 %shard_map.82 = (bf16[4096,128]{1,0:T(8,128)(2,1)S(1)}, bf16[4096,128]{1,0:T(8,128)(2,1)S(1)}, bf16[4096,128]{1,0:T(8,128)(2,1)S(1)}, f32[8,128]{1,0:T(8,128)S(1...) custom-call(s32[5]{0:T(128)S(1)} %stack.32.place_ref.refs_0_.refs_4_.refs_8_, ...), custom_call_target="tpu_custom_call" | custom-call | tf_op jit(solution)/shard_map/pallas_call | solution.py:372
  92.8 2.7 %shard_map.83 = (bf16[4096,128]{1,0:T(8,128)(2,1)S(1)}, bf16[4096,128]{1,0:T(8,128)(2,1)S(1)}, bf16[4096,128]{1,0:T(8,128)(2,1)S(1)}, f32[8,128]{1,0:T(8,128)S(1...) custom-call(s32[5]{0:T(128)S(1)} %stack.32.place_ref.refs_0_.refs_4_.refs_8_, ...), custom_call_target="tpu_custom_call" | custom-call | tf_op jit(solution)/shard_map/pallas_call | solution.py:372
  108.4 9.7 %collective-permute-start.26 = (bf16[2064,128]{1,0:T(8,128)(2,1)S(1)}, bf16[2064,128]{1,0:T(8,128)(2,1)S(1)}, u32[]{:S(2)}, u32[]{:S(2)}) collective-permute-start(bf16[2064,128]{1,0:T(8,128)(2,1)S(1)} %get-tuple-element.209), channel_id=1, source_target_pairs={{0,32},{32,0},{1,33},{33,1},{2,34},{34,2},{3,35},{35,3},{4,36},{36... | collective-permute-start | bytes 1585160 | tf_op jit(solution)/shard_map/ppermute | solution.py:383
  126.8 2.7 %collective-permute-start.32 = (bf16[16,128,128]{2,1,0:T(8,128)(2,1)S(1)}, bf16[16,128,128]{2,1,0:T(8,128)(2,1)S(1)}, u32[]{:S(2)}, u32[]{:S(2)}) collective-permute-start(bf16[16,128,128]{2,1,0:T(8,128)(2,1)S(1)} %get-tuple-element.260), channel_id=1, source_target_pairs={{0,6},{2,0},{4,2},{6,4},{1,7},{3,1},{5,3},{7,5},{8,14},{10,8},{12,... | collective-permute-start | bytes 1572872 | tf_op jit(solution)/shard_map/ppermute | solution.py:387
  129.7 2.7 %collective-permute-start.28 = (bf16[16,128,128]{2,1,0:T(8,128)(2,1)S(1)}, bf16[16,128,128]{2,1,0:T(8,128)(2,1)S(1)}, u32[]{:S(2)}, u32[]{:S(2)}) collective-permute-start(bf16[16,128,128]{2,1,0:T(8,128)(2,1)S(1)} %get-tuple-element.262), channel_id=1, source_target_pairs={{0,24},{8,0},{16,8},{24,16},{1,25},{9,1},{17,9},{25,17},{2,26},{10... | collective-permute-start | bytes 1572872 | tf_op jit(solution)/shard_map/ppermute | solution.py:387
  132.4 9.0 %collective-permute-done.33.hi_ref = bf16[16,128,128]{2,1,0:T(8,128)(2,1)S(1)} collective-permute-done((bf16[16,128,128]{2,1,0:T(8,128)(2,1)S(1)}, bf16[16,128,128]{2,1,0:T(8,128)(2,1)S(1)}, u32[]{:S(2)}, u32[]{:S(2)}) %collective-permute-start.33) | collective-permute-done | bytes 524320 | tf_op jit(solution)/shard_map/ppermute | solution.py:387
  147.6 18.4 %collective-permute-done.34.refs_4_ = bf16[32,128,128]{2,1,0:T(8,128)(2,1)S(1)} collective-permute-done((bf16[32,128,128]{2,1,0:T(8,128)(2,1)S(1)}, bf16[32,128,128]{2,1,0:T(8,128)(2,1)S(1)}, u32[]{:S(2)}, u32[]{:S(2)}) %collective-permute-start.34) | collective-permute-done | bytes 1048608 | tf_op jit(solution)/shard_map/ppermute | solution.py:387
  166.0 3.0 %collective-permute-done.35.refs_5_ = bf16[32,128,128]{2,1,0:T(8,128)(2,1)S(1)} collective-permute-done((bf16[32,128,128]{2,1,0:T(8,128)(2,1)S(1)}, bf16[32,128,128]{2,1,0:T(8,128)(2,1)S(1)}, u32[]{:S(2)}, u32[]{:S(2)}) %collective-permute-start.35) | collective-permute-done | bytes 1048608 | tf_op jit(solution)/shard_map/ppermute | solution.py:387
  168.9 2.7 %collective-permute-done.31.refs_2_ = bf16[32,128,128]{2,1,0:T(8,128)(2,1)S(1)} collective-permute-done((bf16[32,128,128]{2,1,0:T(8,128)(2,1)S(1)}, bf16[32,128,128]{2,1,0:T(8,128)(2,1)S(1)}, u32[]{:S(2)}, u32[]{:S(2)}) %collective-permute-start.31) | collective-permute-done | bytes 1048608 | tf_op jit(solution)/shard_map/ppermute | solution.py:387
  176.9 3.8 %collective-permute-done.36.refs_1_ = bf16[2,4,128,128]{3,2,1,0:T(8,128)(2,1)S(1)} collective-permute-done((bf16[2,4,128,128]{3,2,1,0:T(8,128)(2,1)S(1)}, bf16[2,4,128,128]{3,2,1,0:T(8,128)(2,1)S(1)}, u32[]{:S(2)}, u32[]{:S(2)}) %collective-permute-start.36) | collective-permute-done | bytes 262176 | tf_op jit(solution)/shard_map/ppermute | solution.py:387
  182.2 7.3 %collective-permute-done.38.refs_3_ = bf16[2,4,128,128]{3,2,1,0:T(8,128)(2,1)S(1)} collective-permute-done((bf16[2,4,128,128]{3,2,1,0:T(8,128)(2,1)S(1)}, bf16[2,4,128,128]{3,2,1,0:T(8,128)(2,1)S(1)}, u32[]{:S(2)}, u32[]{:S(2)}) %collective-permute-start.38) | collective-permute-done | bytes 262176 | tf_op jit(solution)/shard_map/ppermute | solution.py:387
  198.6 6.1 %collective-permute-start.45 = (f32[2,128,128]{2,1,0:T(8,128)S(1)}, f32[2,128,128]{2,1,0:T(8,128)S(1)}, u32[]{:S(2)}, u32[]{:S(2)}) collective-permute-start(f32[2,128,128]{2,1,0:T(8,128)S(1)} %get-tuple-element.255), channel_id=1, source_target_pairs={{0,32},{32,0},{1,33},{33,1},{2,34},{34,2},{3,35},{35,3},{4,36},{36... | collective-permute-start | bytes 393224 | tf_op jit(solution)/shard_map/ppermute | solution.py:383
  (117 shorter events, 80.5 us)
Async XLA Ops:
  9.7 9.4 %collective-permute-start.1 = (bf16[2,2,128,128]{3,2,1,0:T(8,128)(2,1)S(1)}, bf16[2,2,128,128]{3,2,1,0:T(8,128)(2,1)S(1)}, u32[]{:S(2)}, u32[]{:S(2)}) collective-permute-start(bf16[2,2,128,128]{3,2,1,0:T(8,128)(2,1)S(1)} %pad_maximum_fusion.p0), channel_id=1, source_target_pairs={{0,1},{1,64},{64,65},{65,0},{2,3},{3,66},{66,67},{67,2},{4,5},{5,6... | collective-permute-start | bytes 393224 | tf_op jit(solution)/shard_map/ppermute | solution.py:387
  19.7 9.0 %collective-permute-start.6 = (bf16[8,128,128]{2,1,0:T(8,128)(2,1)S(1)}, bf16[8,128,128]{2,1,0:T(8,128)(2,1)S(1)}, u32[]{:S(2)}, u32[]{:S(2)}) collective-permute-start(bf16[8,128,128]{2,1,0:T(8,128)(2,1)S(1)} %get-tuple-element.135.refs_0_), channel_id=1, source_target_pairs={{0,6},{2,0},{4,2},{6,4},{1,7},{3,1},{5,3},{7,5},{8,14},{10,8},{12,... | collective-permute-start | bytes 786440 | tf_op jit(solution)/shard_map/ppermute | solution.py:387
  26.0 8.9 %collective-permute-start.8 = (bf16[8,128,128]{2,1,0:T(8,128)(2,1)S(1)}, bf16[8,128,128]{2,1,0:T(8,128)(2,1)S(1)}, u32[]{:S(2)}, u32[]{:S(2)}) collective-permute-start(bf16[8,128,128]{2,1,0:T(8,128)(2,1)S(1)} %get-tuple-element.136.refs_5_), channel_id=1, source_target_pairs={{0,8},{8,16},{16,24},{24,0},{1,9},{9,17},{17,25},{25,1},{2,10},{10... | collective-permute-start | bytes 786440 | tf_op jit(solution)/shard_map/ppermute | solution.py:387
  40.7 21.7 %collective-permute-start.14 = (bf16[32,128,128]{2,1,0:T(8,128)(2,1)S(1)}, bf16[32,128,128]{2,1,0:T(8,128)(2,1)S(1)}, u32[]{:S(2)}, u32[]{:S(2)}) collective-permute-start(bf16[32,128,128]{2,1,0:T(8,128)(2,1)S(1)} %get-tuple-element.137.w0.refs_10_), channel_id=1, source_target_pairs={{0,24},{8,0},{16,8},{24,16},{1,25},{9,1},{17,9},{25,17},{2,26},{10... | collective-permute-start | bytes 3145736 | tf_op jit(solution)/shard_map/ppermute | solution.py:387
  40.8 23.2 %collective-permute-start.12 = (bf16[32,128,128]{2,1,0:T(8,128)(2,1)S(1)}, bf16[32,128,128]{2,1,0:T(8,128)(2,1)S(1)}, u32[]{:S(2)}, u32[]{:S(2)}) collective-permute-start(bf16[32,128,128]{2,1,0:T(8,128)(2,1)S(1)} %get-tuple-element.137.w0.refs_10_), channel_id=1, source_target_pairs={{0,8},{8,16},{16,24},{24,0},{1,9},{9,17},{17,25},{25,1},{2,10},{10... | collective-permute-start | bytes 3145736 | tf_op jit(solution)/shard_map/ppermute | solution.py:387
  42.2 21.9 %collective-permute-start.19 = (bf16[32,128,128]{2,1,0:T(8,128)(2,1)S(1)}, bf16[32,128,128]{2,1,0:T(8,128)(2,1)S(1)}, u32[]{:S(2)}, u32[]{:S(2)}) collective-permute-start(bf16[32,128,128]{2,1,0:T(8,128)(2,1)S(1)} %get-tuple-element.141.l0.refs_15_), channel_id=1, source_target_pairs={{0,6},{2,0},{4,2},{6,4},{1,7},{3,1},{5,3},{7,5},{8,14},{10,8},{12,... | collective-permute-start | bytes 3145736 | tf_op jit(solution)/shard_map/ppermute | solution.py:387
  44.9 22.1 %collective-permute-start.17 = (bf16[32,128,128]{2,1,0:T(8,128)(2,1)S(1)}, bf16[32,128,128]{2,1,0:T(8,128)(2,1)S(1)}, u32[]{:S(2)}, u32[]{:S(2)}) collective-permute-start(bf16[32,128,128]{2,1,0:T(8,128)(2,1)S(1)} %get-tuple-element.141.l0.refs_15_), channel_id=1, source_target_pairs={{0,2},{2,4},{4,6},{6,0},{1,3},{3,5},{5,7},{7,1},{8,10},{10,12},{12... | collective-permute-start | bytes 3145736 | tf_op jit(solution)/shard_map/ppermute | solution.py:387
  62.4 11.0 %collective-permute-start.15 = (bf16[17,128,128]{2,1,0:T(8,128)(2,1)S(1)}, bf16[17,128,128]{2,1,0:T(8,128)(2,1)S(1)}, u32[]{:S(2)}, u32[]{:S(2)}) collective-permute-start(bf16[17,128,128]{2,1,0:T(8,128)(2,1)S(1)} %slice.53), channel_id=1, source_target_pairs={{0,24},{8,0},{16,8},{24,16},{1,25},{9,1},{17,9},{25,17},{2,26},{10... | collective-permute-start | bytes 1671176 | tf_op jit(solution)/shard_map/ppermute | solution.py:387
  64.0 11.4 %collective-permute-start.13 = (bf16[17,128,128]{2,1,0:T(8,128)(2,1)S(1)}, bf16[17,128,128]{2,1,0:T(8,128)(2,1)S(1)}, u32[]{:S(2)}, u32[]{:S(2)}) collective-permute-start(bf16[17,128,128]{2,1,0:T(8,128)(2,1)S(1)} %slice.52), channel_id=1, source_target_pairs={{0,8},{8,16},{16,24},{24,0},{1,9},{9,17},{17,25},{25,1},{2,10},{10... | collective-permute-start | bytes 1671176 | tf_op jit(solution)/shard_map/ppermute | solution.py:387
  64.1 17.4 %collective-permute-start.20 = (bf16[17,128,128]{2,1,0:T(8,128)(2,1)S(1)}, bf16[17,128,128]{2,1,0:T(8,128)(2,1)S(1)}, u32[]{:S(2)}, u32[]{:S(2)}) collective-permute-start(bf16[17,128,128]{2,1,0:T(8,128)(2,1)S(1)} %slice.55), channel_id=1, source_target_pairs={{0,6},{2,0},{4,2},{6,4},{1,7},{3,1},{5,3},{7,5},{8,14},{10,8},{12,... | collective-permute-start | bytes 1671176 | tf_op jit(solution)/shard_map/ppermute | solution.py:387
  67.0 14.5 %collective-permute-start.18 = (bf16[17,128,128]{2,1,0:T(8,128)(2,1)S(1)}, bf16[17,128,128]{2,1,0:T(8,128)(2,1)S(1)}, u32[]{:S(2)}, u32[]{:S(2)}) collective-permute-start(bf16[17,128,128]{2,1,0:T(8,128)(2,1)S(1)} %slice.54), channel_id=1, source_target_pairs={{0,2},{2,4},{4,6},{6,0},{1,3},{3,5},{5,7},{7,1},{8,10},{10,12},{12... | collective-permute-start | bytes 1671176 | tf_op jit(solution)/shard_map/ppermute | solution.py:387
  108.4 11.9 %collective-permute-start.26 = (bf16[2064,128]{1,0:T(8,128)(2,1)S(1)}, bf16[2064,128]{1,0:T(8,128)(2,1)S(1)}, u32[]{:S(2)}, u32[]{:S(2)}) collective-permute-start(bf16[2064,128]{1,0:T(8,128)(2,1)S(1)} %get-tuple-element.209), channel_id=1, source_target_pairs={{0,32},{32,0},{1,33},{33,1},{2,34},{34,2},{3,35},{35,3},{4,36},{36... | collective-permute-start | bytes 1585160 | tf_op jit(solution)/shard_map/ppermute | solution.py:383
  126.8 14.6 %collective-permute-start.33 = (bf16[16,128,128]{2,1,0:T(8,128)(2,1)S(1)}, bf16[16,128,128]{2,1,0:T(8,128)(2,1)S(1)}, u32[]{:S(2)}, u32[]{:S(2)}) collective-permute-start(bf16[16,128,128]{2,1,0:T(8,128)(2,1)S(1)} %get-tuple-element.259), channel_id=1, source_target_pairs={{0,2},{2,4},{4,6},{6,0},{1,3},{3,5},{5,7},{7,1},{8,10},{10,12},{12... | collective-permute-start | bytes 1572872 | tf_op jit(solution)/shard_map/ppermute | solution.py:387
  126.8 14.6 %collective-permute-start.32 = (bf16[16,128,128]{2,1,0:T(8,128)(2,1)S(1)}, bf16[16,128,128]{2,1,0:T(8,128)(2,1)S(1)}, u32[]{:S(2)}, u32[]{:S(2)}) collective-permute-start(bf16[16,128,128]{2,1,0:T(8,128)(2,1)S(1)} %get-tuple-element.260), channel_id=1, source_target_pairs={{0,6},{2,0},{4,2},{6,4},{1,7},{3,1},{5,3},{7,5},{8,14},{10,8},{12,... | collective-permute-start | bytes 1572872 | tf_op jit(solution)/shard_map/ppermute | solution.py:387
  129.6 15.0 %collective-permute-start.29 = (bf16[16,128,128]{2,1,0:T(8,128)(2,1)S(1)}, bf16[16,128,128]{2,1,0:T(8,128)(2,1)S(1)}, u32[]{:S(2)}, u32[]{:S(2)}) collective-permute-start(bf16[16,128,128]{2,1,0:T(8,128)(2,1)S(1)} %get-tuple-element.261), channel_id=1, source_target_pairs={{0,8},{8,16},{16,24},{24,0},{1,9},{9,17},{17,25},{25,1},{2,10},{10... | collective-permute-start | bytes 1572872 | tf_op jit(solution)/shard_map/ppermute | solution.py:387
  129.7 15.0 %collective-permute-start.28 = (bf16[16,128,128]{2,1,0:T(8,128)(2,1)S(1)}, bf16[16,128,128]{2,1,0:T(8,128)(2,1)S(1)}, u32[]{:S(2)}, u32[]{:S(2)}) collective-permute-start(bf16[16,128,128]{2,1,0:T(8,128)(2,1)S(1)} %get-tuple-element.262), channel_id=1, source_target_pairs={{0,24},{8,0},{16,8},{24,16},{1,25},{9,1},{17,9},{25,17},{2,26},{10... | collective-permute-start | bytes 1572872 | tf_op jit(solution)/shard_map/ppermute | solution.py:387
  142.2 23.8 %collective-permute-start.34 = (bf16[32,128,128]{2,1,0:T(8,128)(2,1)S(1)}, bf16[32,128,128]{2,1,0:T(8,128)(2,1)S(1)}, u32[]{:S(2)}, u32[]{:S(2)}) collective-permute-start(bf16[32,128,128]{2,1,0:T(8,128)(2,1)S(1)} %get-tuple-element.240), channel_id=1, source_target_pairs={{0,6},{2,0},{4,2},{6,4},{1,7},{3,1},{5,3},{7,5},{8,14},{10,8},{12,... | collective-permute-start | bytes 3145736 | tf_op jit(solution)/shard_map/ppermute | solution.py:387
  144.6 24.3 %collective-permute-start.35 = (bf16[32,128,128]{2,1,0:T(8,128)(2,1)S(1)}, bf16[32,128,128]{2,1,0:T(8,128)(2,1)S(1)}, u32[]{:S(2)}, u32[]{:S(2)}) collective-permute-start(bf16[32,128,128]{2,1,0:T(8,128)(2,1)S(1)} %get-tuple-element.241), channel_id=1, source_target_pairs={{0,2},{2,4},{4,6},{6,0},{1,3},{3,5},{5,7},{7,1},{8,10},{10,12},{12... | collective-permute-start | bytes 3145736 | tf_op jit(solution)/shard_map/ppermute | solution.py:387
  145.5 23.5 %collective-permute-start.30 = (bf16[32,128,128]{2,1,0:T(8,128)(2,1)S(1)}, bf16[32,128,128]{2,1,0:T(8,128)(2,1)S(1)}, u32[]{:S(2)}, u32[]{:S(2)}) collective-permute-start(bf16[32,128,128]{2,1,0:T(8,128)(2,1)S(1)} %get-tuple-element.234), channel_id=1, source_target_pairs={{0,24},{8,0},{16,8},{24,16},{1,25},{9,1},{17,9},{25,17},{2,26},{10... | collective-permute-start | bytes 3145736 | tf_op jit(solution)/shard_map/ppermute | solution.py:387
  147.6 24.0 %collective-permute-start.31 = (bf16[32,128,128]{2,1,0:T(8,128)(2,1)S(1)}, bf16[32,128,128]{2,1,0:T(8,128)(2,1)S(1)}, u32[]{:S(2)}, u32[]{:S(2)}) collective-permute-start(bf16[32,128,128]{2,1,0:T(8,128)(2,1)S(1)} %get-tuple-element.235), channel_id=1, source_target_pairs={{0,8},{8,16},{16,24},{24,0},{1,9},{9,17},{17,25},{25,1},{2,10},{10... | collective-permute-start | bytes 3145736 | tf_op jit(solution)/shard_map/ppermute | solution.py:387
  175.4 14.1 %collective-permute-start.38 = (bf16[2,4,128,128]{3,2,1,0:T(8,128)(2,1)S(1)}, bf16[2,4,128,128]{3,2,1,0:T(8,128)(2,1)S(1)}, u32[]{:S(2)}, u32[]{:S(2)}) collective-permute-start(bf16[2,4,128,128]{3,2,1,0:T(8,128)(2,1)S(1)} %get-tuple-element.245), channel_id=1, source_target_pairs={{0,2},{2,4},{4,6},{6,0},{1,3},{3,5},{5,7},{7,1},{8,10},{10,12},{12... | collective-permute-start | bytes 786440 | tf_op jit(solution)/shard_map/ppermute | solution.py:387
  176.0 13.5 %collective-permute-start.39 = (bf16[2,4,128,128]{3,2,1,0:T(8,128)(2,1)S(1)}, bf16[2,4,128,128]{3,2,1,0:T(8,128)(2,1)S(1)}, u32[]{:S(2)}, u32[]{:S(2)}) collective-permute-start(bf16[2,4,128,128]{3,2,1,0:T(8,128)(2,1)S(1)} %get-tuple-element.247), channel_id=1, source_target_pairs={{0,24},{8,0},{16,8},{24,16},{1,25},{9,1},{17,9},{25,17},{2,26},{10... | collective-permute-start | bytes 786440 | tf_op jit(solution)/shard_map/ppermute | solution.py:387
  176.3 13.2 %collective-permute-start.40 = (bf16[2,4,128,128]{3,2,1,0:T(8,128)(2,1)S(1)}, bf16[2,4,128,128]{3,2,1,0:T(8,128)(2,1)S(1)}, u32[]{:S(2)}, u32[]{:S(2)}) collective-permute-start(bf16[2,4,128,128]{3,2,1,0:T(8,128)(2,1)S(1)} %get-tuple-element.248), channel_id=1, source_target_pairs={{0,16},{8,24},{16,0},{24,8},{1,17},{9,25},{17,1},{25,9},{2,18},{10... | collective-permute-start | bytes 786440 | tf_op jit(solution)/shard_map/ppermute | solution.py:387
  180.7 9.5 %collective-permute-start.41 = (bf16[2,4,128,128]{3,2,1,0:T(8,128)(2,1)S(1)}, bf16[2,4,128,128]{3,2,1,0:T(8,128)(2,1)S(1)}, u32[]{:S(2)}, u32[]{:S(2)}) collective-permute-start(bf16[2,4,128,128]{3,2,1,0:T(8,128)(2,1)S(1)} %get-tuple-element.249), channel_id=1, source_target_pairs={{0,8},{8,16},{16,24},{24,0},{1,9},{9,17},{17,25},{25,1},{2,10},{10... | collective-permute-start | bytes 786440 | tf_op jit(solution)/shard_map/ppermute | solution.py:387
  (29 other events, 352.9 us)
